TPU v7x, 128 devices: a whole 4x4x4 slice. The times are simulated.
128 devices in a mesh: dp: 16 (over z_hi, x, core), tensor: 8 (over z_lo, y).
Axes of the slice: x: 4, y: 4, z: 4 (z_hi: 2, z_lo: 2; z = z_hi * 2 + z_lo), core: 2. Of those that a mesh axis runs over, the one named last changes fastest.
Arguments:
- tokens: bfloat16 [16384, 2048], P('dp'), may hold values from -6 to 6
- cotangent: bfloat16 [16384, 2048], P('dp'), may hold values from -6 to 6
- seq_lengths: int32 [16, 8], P('dp'), may hold values from 0 to 1024, as said below
- ln_gain: bfloat16 [2048], replicated, may hold values from 0.5 to 1.5
- ln_bias: bfloat16 [2048], replicated, may hold values from -1.75 to 1.75
- w_qkv: bfloat16 [2048, 6144], P(None, 'tensor'), may hold values from -0.125 to 0.125
- b_qkv: bfloat16 [6144], P('tensor'), may hold values from -3 to 3
- w_dense: bfloat16 [2048, 2048], P('tensor'), may hold values from -0.5 to 0.5
- b_dense: bfloat16 [2048], replicated, may hold values from -1.75 to 1.75
- w_fc1: bfloat16 [2048, 8192], P(None, 'tensor'), may hold values from -0.125 to 0.125
- b_fc1: bfloat16 [8192], P('tensor'), may hold values from -3 to 3
- w_fc2: bfloat16 [8192, 2048], P('tensor'), may hold values from -0.0625 to 0.0625
- b_fc2: bfloat16 [2048], replicated, may hold values from -1.75 to 1.75
Outputs:
- output: bfloat16 [16384, 2048], P('dp')
- grad_tokens: bfloat16 [16384, 2048], P('dp')
- grad_ln_gain: float32 [2048], P('dp')
- grad_ln_bias: float32 [2048], P('dp')
- grad_w_qkv: float32 [2048, 6144], P('dp', 'tensor')
- grad_b_qkv: float32 [6144], P(('tensor', 'dp'))
- grad_w_dense: float32 [2048, 2048], P('tensor', 'dp')
- grad_b_dense: float32 [2048], P('dp')
- grad_w_fc1: float32 [2048, 8192], P('dp', 'tensor')
- grad_b_fc1: float32 [8192], P(('tensor', 'dp'))
- grad_w_fc2: float32 [8192, 2048], P('tensor', 'dp')
- grad_b_fc2: float32 [2048], P('dp')
Inputs may be any that keep to these rules, and one draw needn't show every extreme that they name: `seq_lengths`: row r lists the lengths of the sequences packed in order from the start of slot r of 1024 positions; the rest of the slot is padding and zero entries are unused places. In every draw one row is a single sequence of exactly 1024.
All inputs are finite; a program needn't handle non-finite values.
Results may differ from a plain program's by a relative error of at most 0.014.
Values may be sent and summed in bfloat16 or wider, within the bound.
No kernel may reach another device: no remote copies, remote signals or barrier semaphores. Data moves between devices by JAX's collectives and lax.ppermute only.
A program may use at most 192 MiB of HBM per device.

v0:
```python
from functools import partial

import jax
import jax.numpy as jnp
from jax import lax
from jax.sharding import PartitionSpec as P

HEAD_DIM = 64
ROTARY = 32


def slot_layout(lengths_row, slot_len):
    places = jnp.arange(slot_len, dtype=jnp.int32)
    seq_ends = jnp.cumsum(lengths_row)
    segment = jnp.sum((places[:, None] >= seq_ends[None, :]).astype(jnp.int32), axis=1)
    starts = jnp.concatenate([jnp.zeros((1,), jnp.int32), seq_ends])
    picked = segment[:, None] == jnp.arange(starts.shape[0], dtype=jnp.int32)[None, :]
    position = places - jnp.sum(jnp.where(picked, starts[None, :], 0), axis=1)
    valid_rows = (places < seq_ends[-1]).astype(jnp.float32)
    return (segment, position, valid_rows)


def rotary_tables(position):
    half_rot = ROTARY // 2
    frequency = 10000.0 ** (-jnp.arange(half_rot, dtype=jnp.float32) * 2.0 / ROTARY)
    angles = position.astype(jnp.float32)[:, None] * frequency[None, :]
    cosines = jnp.concatenate([jnp.cos(angles), jnp.cos(angles)], axis=1)
    sines = jnp.concatenate([jnp.sin(angles), jnp.sin(angles)], axis=1)
    return (cosines, sines)


def rotate(heads_in, cosines, sines):
    half_rot = ROTARY // 2
    rotary = heads_in[..., :ROTARY]
    turned = jnp.concatenate([-rotary[..., half_rot:ROTARY], rotary[..., :half_rot]], axis=-1)
    mixed_rot = rotary * cosines[:, None, :] + turned * sines[:, None, :]
    return jnp.concatenate([mixed_rot, heads_in[..., ROTARY:]], axis=-1)


def norm_backward(grad_rows, normed_rows, inv_rows, upstream_rows, norm_gain):
    scaled = grad_rows * norm_gain
    input_part = inv_rows * (
        scaled
        - jnp.mean(scaled, axis=1, keepdims=True)
        - normed_rows * jnp.mean(scaled * normed_rows, axis=1, keepdims=True)
    )
    return (
        (upstream_rows + input_part).astype(jnp.bfloat16),
        jnp.sum(grad_rows * normed_rows, axis=0),
        jnp.sum(grad_rows, axis=0),
    )


def per_device(
    tokens,
    cotangent,
    seq_lengths,
    ln_gain,
    ln_bias,
    w_qkv,
    b_qkv,
    w_dense,
    b_dense,
    w_fc1,
    b_fc1,
    w_fc2,
    b_fc2,
):
    slot_len = tokens.shape[0]
    local_heads = w_dense.shape[0] // HEAD_DIM
    score_scale = HEAD_DIM ** (-0.5)
    segment, position, valid_rows = slot_layout(seq_lengths[0], slot_len)
    cosines, sines = rotary_tables(position)
    places = jnp.arange(slot_len, dtype=jnp.int32)
    allowed = (segment[:, None] == segment[None, :]) & (places[:, None] >= places[None, :])
    inputs = tokens.astype(jnp.float32)
    center = inputs - jnp.mean(inputs, axis=1, keepdims=True)
    inv_sigma = lax.rsqrt(jnp.mean(center * center, axis=1, keepdims=True) + 1e-05)
    normed = center * inv_sigma
    norm_gain = ln_gain.astype(jnp.float32)
    hidden = (normed * norm_gain + ln_bias.astype(jnp.float32)).astype(jnp.bfloat16)
    projected = jnp.dot(hidden, w_qkv, preferred_element_type=jnp.float32) + b_qkv.astype(
        jnp.float32
    )
    projected = projected.reshape(slot_len, local_heads, 3, HEAD_DIM)
    query_pre = projected[:, :, 0]
    key_pre = projected[:, :, 1]
    queries = rotate(query_pre, cosines, sines).astype(jnp.bfloat16)
    keys_in = rotate(key_pre, cosines, sines).astype(jnp.bfloat16)
    values = projected[:, :, 2].astype(jnp.bfloat16)

    def masked_scores():
        scores = (
            jnp.einsum("qhd,khd->hqk", queries, keys_in, preferred_element_type=jnp.float32)
            * score_scale
        )
        return jnp.where(allowed[None], scores, -1e30)

    scores = masked_scores()
    row_max = jnp.max(scores, axis=2, keepdims=True)
    log_total = row_max + jnp.log(jnp.sum(jnp.exp(scores - row_max), axis=2, keepdims=True))
    softmax_out = jnp.exp(scores - log_total)
    context = jnp.einsum(
        "hqk,khd->qhd", softmax_out.astype(jnp.bfloat16), values, preferred_element_type=jnp.float32
    )
    context = context.reshape(slot_len, local_heads * HEAD_DIM).astype(jnp.bfloat16)
    attn_part = jnp.dot(context, w_dense, preferred_element_type=jnp.float32)
    up_pre = jnp.dot(hidden, w_fc1, preferred_element_type=jnp.float32) + b_fc1.astype(jnp.float32)
    activated = jax.nn.gelu(up_pre, approximate=True).astype(jnp.bfloat16)
    mlp_part = jnp.dot(activated, w_fc2, preferred_element_type=jnp.float32)
    bias_sum = b_dense.astype(jnp.float32) + b_fc2.astype(jnp.float32)
    branch = lax.psum((attn_part + mlp_part).astype(jnp.bfloat16), "tensor").astype(jnp.float32)
    output = (inputs + valid_rows[:, None] * (branch + bias_sum)).astype(jnp.bfloat16)
    upstream = cotangent.astype(jnp.float32)
    branch_grad = (valid_rows[:, None] * upstream).astype(jnp.bfloat16)
    bias_grad = jnp.sum(branch_grad.astype(jnp.float32), axis=0)
    grad_fc2 = jnp.einsum("tf,td->fd", activated, branch_grad, preferred_element_type=jnp.float32)
    act_grad = jnp.einsum("td,fd->tf", branch_grad, w_fc2, preferred_element_type=jnp.float32)
    unused_out, gelu_pullback = jax.vjp(partial(jax.nn.gelu, approximate=True), up_pre)
    up_grad = gelu_pullback(act_grad)[0].astype(jnp.bfloat16)
    grad_fc1 = jnp.einsum("tc,tf->cf", hidden, up_grad, preferred_element_type=jnp.float32)
    grad_b_fc1 = jnp.sum(up_grad.astype(jnp.float32), axis=0)
    hidden_grad = jnp.einsum("tf,cf->tc", up_grad, w_fc1, preferred_element_type=jnp.float32)
    grad_dense = jnp.einsum("tc,td->cd", context, branch_grad, preferred_element_type=jnp.float32)
    context_grad = jnp.einsum("td,cd->tc", branch_grad, w_dense, preferred_element_type=jnp.float32)
    context_grad = context_grad.astype(jnp.bfloat16).reshape(slot_len, local_heads, HEAD_DIM)
    again_scores = masked_scores()
    again_softmax = jnp.exp(again_scores - log_total)
    prob_grad = jnp.einsum("qhd,khd->hqk", context_grad, values, preferred_element_type=jnp.float32)
    value_grad = jnp.einsum(
        "hqk,qhd->khd",
        again_softmax.astype(jnp.bfloat16),
        context_grad,
        preferred_element_type=jnp.float32,
    )
    row_dot = jnp.sum(prob_grad * again_softmax, axis=2, keepdims=True)
    score_grad = (again_softmax * (prob_grad - row_dot)).astype(jnp.bfloat16)
    query_grad = (
        jnp.einsum("hqk,khd->qhd", score_grad, keys_in, preferred_element_type=jnp.float32)
        * score_scale
    )
    key_grad = (
        jnp.einsum("hqk,qhd->khd", score_grad, queries, preferred_element_type=jnp.float32)
        * score_scale
    )
    unused_pair, rotary_pullback = jax.vjp(
        lambda first, second: (rotate(first, cosines, sines), rotate(second, cosines, sines)),
        query_pre,
        key_pre,
    )
    query_pre_grad, key_pre_grad = rotary_pullback((query_grad, key_grad))
    projected_grad = (
        jnp.stack([query_pre_grad, key_pre_grad, value_grad], axis=2)
        .reshape(slot_len, local_heads * 3 * HEAD_DIM)
        .astype(jnp.bfloat16)
    )
    grad_qkv = jnp.einsum("tc,tf->cf", hidden, projected_grad, preferred_element_type=jnp.float32)
    grad_b_qkv = jnp.sum(projected_grad.astype(jnp.float32), axis=0)
    hidden_grad = hidden_grad + jnp.einsum(
        "tf,cf->tc", projected_grad, w_qkv, preferred_element_type=jnp.float32
    )
    whole_grad = lax.psum(hidden_grad.astype(jnp.bfloat16), "tensor").astype(jnp.float32)
    input_grad, gain_grad, shift_grad = norm_backward(
        whole_grad, normed, inv_sigma, upstream, norm_gain
    )
    summed = (
        lax.psum_scatter(grad_qkv, "dp", scatter_dimension=0, tiled=True),
        lax.psum_scatter(grad_b_qkv, "dp", scatter_dimension=0, tiled=True),
        lax.psum_scatter(grad_dense, "dp", scatter_dimension=1, tiled=True),
        lax.psum_scatter(bias_grad, "dp", scatter_dimension=0, tiled=True),
        lax.psum_scatter(grad_fc1, "dp", scatter_dimension=0, tiled=True),
        lax.psum_scatter(grad_b_fc1, "dp", scatter_dimension=0, tiled=True),
        lax.psum_scatter(grad_fc2, "dp", scatter_dimension=1, tiled=True),
        lax.psum_scatter(gain_grad, "dp", scatter_dimension=0, tiled=True),
        lax.psum_scatter(shift_grad, "dp", scatter_dimension=0, tiled=True),
    )
    out_qkv, out_b_qkv, out_dense, out_bias, out_fc1, out_b_fc1, out_fc2, out_gain, out_shift = (
        summed
    )
    return (
        output,
        input_grad,
        out_gain,
        out_shift,
        out_qkv,
        out_b_qkv,
        out_dense,
        out_bias,
        out_fc1,
        out_b_fc1,
        out_fc2,
        out_bias,
    )


def solution(mesh):
    placed = (
        P("dp", None),
        P("dp", None),
        P("dp", None),
        P(),
        P(),
        P(None, "tensor"),
        P("tensor"),
        P("tensor", None),
        P(),
        P(None, "tensor"),
        P("tensor"),
        P("tensor", None),
        P(),
    )
    return jax.shard_map(
        per_device,
        mesh=mesh,
        in_specs=placed,
        out_specs=(
            P("dp", None),
            P("dp", None),
            P("dp"),
            P("dp"),
            P("dp", "tensor"),
            P(("tensor", "dp")),
            P("tensor", "dp"),
            P("dp"),
            P("dp", "tensor"),
            P(("tensor", "dp")),
            P("tensor", "dp"),
            P("dp"),
        ),
        check_vma=False,
    )
```

profile of v0, /device:TPU:0, one launch (start us, length us, event | category | flops | bytes accessed | tf_op | source)
XLA Modules:
  0.0 637.0 jit_solution(4832395724570769520)
XLA Ops:
  8.1 3.0 convert_reduce_fusion.1
  11.1 0.6 copy-done.2
  11.7 1.2 fusion.13
  13.0 0.5 copy-done.30
  13.5 1.8 fusion.10
  15.4 3.6 convolution_add_fusion
  19.0 0.1 fusion.54
  19.2 0.2 copy_bitcast_fusion
  19.4 1.3 copy-done.10
  20.7 0.9 slice_negate_fusion.2
  21.6 0.2 copy-done.5
  21.9 0.9 slice_negate_fusion.3
  22.8 0.7 slice.82
  23.5 0.2 reduce-window.4
  23.7 0.6 slice.44
  24.3 0.1 convert_reduce_fusion.5
  24.5 0.6 fusion.26
  25.1 0.1 select_reduce_fusion
  25.2 0.3 multiply_cosine_fusion
  25.5 1.9 fusion.33
  27.4 3.0 fusion
  30.5 3.7 exponential_reduce_fusion
  34.2 3.8 copy-done.1
  37.9 0.7 fusion.38
  38.6 1.4 convolution_convert_fusion.1
  40.0 0.5 copy-done.11
  40.5 12.2 %multiply_reduce_fusion = (f32[4,1024]{1,0:T(4,128)S(1)}, f32[4,1024,1024]{1,2,0:T(8,128)}) fusion(f32[4,1024,1024]{1,2,0:T(8,128)} %copy-done.1, f32[4,1024]{1,0:T(4,128)S(1)} %log_add_fusion, pred[1024,1024]{0,1:T(8,128)(4,1)S(1)} %fusion.26, bf16[1024,4,64]{0,2,1:T(8,128)(2,1)S(1)} %bitcast.59, f32[1024,4,3,64]{0,3,2,1:T(8,128)S(1)} %bitcast.55), kind=kOutput, calls=%fused_computation.1 | convolution fusion | flops 557838336 | bytes 35684352 | tf_op jit(solution)/shard_map/qhd,khd->hqk/dot_general | solution.py:129
  52.8 12.1 %multiply_convert_fusion = bf16[4,1024,1024]{1,2,0:T(8,128)(2,1)S(1)} fusion(f32[4,1024,1024]{1,2,0:T(8,128)} %get-tuple-element.51, f32[4,1024,1024]{1,2,0:T(8,128)} %copy-done.1, f32[4,1024]{1,0:T(4,128)S(1)} %get-tuple-element.50, f32[4,1024]{1,0:T(4,128)S(1)} %log_add_fusion, pred[1024,1024]{0,1:T(8,128)(4,1)S(1)} %fusion.26), kind=kLoop, calls=%fused_computation | loop fusion | flops 25165824 | bytes 43024384 | tf_op jit(solution)/shard_map/convert_element_type | solution.py:137
  64.9 2.7 fusion.27
  67.6 1.6 fusion.28
  69.1 8.9 %convolution_bitcast_fusion = bf16[1024,4,1,64]{0,3,1,2:T(8,128)(2,1)} fusion(bf16[1024,4,64]{0,2,1:T(8,128)(2,1)S(1)} %bitcast.60, f32[4,1024,1024]{1,2,0:T(8,128)} %copy-done.1, f32[4,1024]{1,0:T(4,128)S(1)} %log_add_fusion, pred[1024,1024]{0,1:T(8,128)(4,1)S(1)} %fusion.26), kind=kOutput, calls=%fused_computation.51 | convolution fusion | flops 553648128 | bytes 18890752 | tf_op jit(solution)/shard_map/hqk,qhd->khd/dot_general | solution.py:130
  78.1 9.0 %convolution_convert_fusion = bf16[4,64,1024]{2,1,0:T(8,128)(2,1)} fusion(f32[4,1024,1024]{1,2,0:T(8,128)} %copy-done.1, f32[4,1024]{1,0:T(4,128)S(1)} %log_add_fusion, pred[1024,1024]{0,1:T(8,128)(4,1)S(1)} %fusion.26, f32[1024,4,3,64]{0,3,2,1:T(8,128)S(1)} %bitcast.56), kind=kOutput, calls=%fused_computation.56 | convolution fusion | flops 553910272 | bytes 18890752 | tf_op jit(solution)/shard_map/hqk,khd->qhd/dot_general | solution.py:103
  87.1 6.2 fusion.59
  93.3 10.0 %convert_reduce_fusion.3 = (f32[1024]{0:T(1024)S(1)}, bf16[1024,1024]{1,0:T(8,128)(2,1)}) fusion(f32[1024,1024]{1,0:T(8,128)} %fusion.59, f32[1024]{0:T(1024)S(1)} %convert_element_type.126, bf16[1024,2048]{1,0:T(8,128)(2,1)S(1)} %copy-done.38, bf16[1024,2048]{1,0:T(8,128)(2,1)S(1)} %copy-done.7, f32[1024]{0:T(1024)S(1)} %fusion.38), kind=kOutput, calls=%fused_computation.44 | convolution fusion | flops 4325374976 | bytes 14692352 | tf_op jit(solution)/shard_map/td,fd->tf/dot_general | solution.py:118
  103.3 6.9 %fusion.45 = f32[1024,2048]{1,0:T(8,128)S(1)} fusion(bf16[1024,2048]{1,0:T(8,128)(2,1)S(1)} %copy-done.38, f32[1024,1024]{1,0:T(8,128)} %fusion.59, f32[1024]{0:T(1024)S(1)} %convert_element_type.126), kind=kOutput, calls=%fused_computation.109 | convolution fusion | flops 4305453056 | bytes 16781312 | tf_op jit(solution)/shard_map/dot_general | solution.py:110
  110.3 0.1 fusion.56
  110.5 0.6 copy-done.16
  111.2 0.2 pad_add_fusion.1
  111.5 0.3 convert_reduce_fusion.4
  111.8 0.2 copy.56
  112.0 2.2 copy-done.40
  114.2 0.7 copy-done.44
  114.9 4.5 fusion.60
  119.5 5.4 add_convert_fusion
  124.8 3.3 add_convert_fusion.1
  128.2 5.1 fusion.47
  133.3 8.9 %fusion.61 = f32[2048,768]{1,0:T(8,128)} fusion(bf16[1024,2048]{1,0:T(8,128)(2,1)} %copy-done.8, bf16[1024,768]{0,1:T(8,128)(2,1)} %bitcast.58), kind=kOutput, calls=%fused_computation.119 | convolution fusion | flops 3221225472 | bytes 12058624 | tf_op jit(solution)/shard_map/tc,tf->cf/dot_general | solution.py:157
  142.3 10.8 %fusion.62 = f32[2048,1024]{1,0:T(8,128)} fusion(bf16[1024,2048]{1,0:T(8,128)(2,1)} %copy-done.8, bf16[1024,1024]{1,0:T(8,128)(2,1)} %get-tuple-element.53), kind=kOutput, calls=%fused_computation.120 | convolution fusion | flops 4294967296 | bytes 14680064 | tf_op jit(solution)/shard_map/tc,tf->cf/dot_general | solution.py:121
  153.1 0.3 reduce-scatter.11.cloned.1.call-start
  153.4 12.7 %fusion.44 = f32[1024,2048]{1,0:T(8,128)} fusion(f32[1024,1024]{1,0:T(8,128)} %fusion.59, f32[1024]{0:T(1024)S(1)} %convert_element_type.126, bf16[1024,2048]{1,0:T(8,128)(2,1)} %param.14, f32[1024]{0:T(1024)S(1)} %fusion.38), kind=kOutput, calls=%fused_computation.108 | convolution fusion | flops 4311744512 | bytes 16785408 | tf_op jit(solution)/shard_map/tf,td->fd/dot_general | solution.py:117
  166.2 0.5 copy-done.42
  166.7 0.6 dynamic-slice
  169.3 146.3 %all-reduce.17.cloned.1.call-done = (bf16[1024,2048]{1,0:T(8,128)(2,1)}, bf16[1024,2048]{1,0:T(8,128)(2,1)}) async-done(((bf16[1024,2048]{1,0:T(8,128)(2,1)}, bf16[1024,2048]{1,0:T(8,128)(2,1)}), (bf16[1024,2048]{1,0:T(8,128)(2,1)}, bf16[1024,2048]{1,0:T(8,128)(2,1)})) %all-reduce.17.cloned.1.call-update) | async-done | bytes 8388624 | tf_op jit(solution)/shard_map/psum | solution.py:112
  315.6 6.4 fusion.18
  322.0 11.5 %convert_reduce_fusion.2 = (f32[2048]{0:T(1024)S(1)}, bf16[1024,2048]{1,0:T(8,128)(2,1)}, bf16[1024,2048]{1,0:T(8,128)(2,1)}) fusion(bf16[1024,2048]{1,0:T(8,128)(2,1)} %param.14, f32[1024]{0:T(1024)S(1)} %fusion.38, f32[1024]{0:T(1024)S(1)} %broadcast_multiply_fusion, f32[1024]{0:T(1024)S(1)} %copy-done.29, bf16[1024,2048]{1,0:T(8,128)(2,1)S(1)} %copy-done.3, ...), kind=kLoop, calls=%fused_computation.32 | loop fusion | flops 44038144 | bytes 25210880 | tf_op jit(solution)/shard_map/reduce_sum | solution.py:116
  333.5 69.6 %all-reduce.13 = (f32[2048]{0:T(1024)S(1)}, f32[2048]{0:T(1024)S(1)}, f32[768]{0:T(1024)S(1)}, f32[2048]{0:T(1024)S(1)}, f32[1024]{0:T(1024)S(1)}) all-reduce(f32[2048]{0:T(1024)S(1)} %get-tuple-element.12, f32[2048]{0:T(1024)S(1)} %get-tuple-element.15, f32[768]{0:T(1024)S(1)} %reduce_sum.130, ...), channel_id=2, replica_groups=mesh['dp'=16,'tensor'=8] {'dp'}, use_global_device_ids=true, to_apply=%region_13.14.clone | all-reduce | flops 7936 | bytes 63488
  403.1 0.6 dynamic-slice.1
  403.7 0.6 dynamic-slice.3
  404.3 0.6 dynamic-slice.5
  404.8 0.6 dynamic-slice.9
  405.4 11.5 %reduce-scatter.5.cloned.1.call-done = f32[128,768]{1,0:T(8,128)} async-done(((f32[2048,768]{1,0:T(8,128)}), f32[128,768]{1,0:T(8,128)}) %reduce-scatter.5.cloned.1.call-update) | async-done | bytes 393232 | tf_op jit(solution)/shard_map/reduce_scatter | solution.py:167
  417.0 105.6 %reduce-scatter.9.cloned.1.call-done = f32[128,1024]{1,0:T(8,128)} async-done(((f32[2048,1024]{1,0:T(8,128)}), f32[128,1024]{1,0:T(8,128)}) %reduce-scatter.9.cloned.1.call-update) | async-done | bytes 524304 | tf_op jit(solution)/shard_map/reduce_scatter | solution.py:171
  522.6 105.8 %reduce-scatter.11.cloned.1.call-done = f32[1024,128]{1,0:T(8,128)} async-done(((f32[1024,2048]{1,0:T(8,128)}), f32[1024,128]{1,0:T(8,128)}) %reduce-scatter.11.cloned.1.call-update) | async-done | bytes 524304 | tf_op jit(solution)/shard_map/reduce_scatter | solution.py:173
  628.4 0.5 copy.77
  (113 shorter events, 1.2 us)
Async XLA Ops:
  8.0 7.4 %copy-start = (bf16[2048,768]{1,0:T(8,128)(2,1)S(1)}, bf16[2048,768]{1,0:T(8,128)(2,1)}, u32[]{:S(2)}) copy-start(bf16[2048,768]{1,0:T(8,128)(2,1)} %param.18) | copy-start | bytes 9437188
  8.0 307.5 %all-reduce.17.cloned.1.call-start = ((), (), s32[]{:S(2)}) async-start(), calls=%async_computation.8 | async-start | bytes 16777216 | tf_op jit(solution)/shard_map/psum | solution.py:112
  8.1 3.6 copy-start.2
  8.1 4.8 copy-start.32
  8.1 4.8 copy-start.33
  8.1 4.9 copy-start.36
  11.7 1.3 copy-start.28
  12.9 0.6 copy-start.30
  13.0 0.6 copy-start.26
  15.4 3.6 copy-start.8
  19.0 1.7 copy-start.10
  19.2 4.4 copy-start.41
  20.7 1.2 copy-start.5
  20.7 2.1 copy-start.6
  21.9 8.6 %copy-start.19 = (bf16[1024,4,32]{0,2,1:T(8,128)(2,1)}, bf16[1024,4,32]{0,2,1:T(8,128)(2,1)S(1)}, u32[]{:S(2)}) copy-start(bf16[1024,4,32]{0,2,1:T(8,128)(2,1)S(1)} %slice.81) | copy-start | bytes 786436
  23.7 3.7 copy-start.21
  25.5 1.9 copy-start.12
  25.5 1.9 copy-start.15
  27.4 3.1 copy-start.22
  30.5 7.5 %copy-start.1 = (f32[4,1024,1024]{1,2,0:T(8,128)}, f32[4,1024,1024]{1,2,0:T(8,128)S(1)}, u32[]{:S(2)}) copy-start(f32[4,1024,1024]{1,2,0:T(8,128)S(1)} %get-tuple-element.49) | copy-start | bytes 50331652
  30.5 8.1 %copy-start.7 = (bf16[1024,2048]{1,0:T(8,128)(2,1)S(1)}, bf16[1024,2048]{1,0:T(8,128)(2,1)}, u32[]{:S(2)}) copy-start(bf16[1024,2048]{1,0:T(8,128)(2,1)} %param.14) | copy-start | bytes 12582916
  30.5 8.1 %copy-start.17 = (bf16[256,2048]{1,0:T(8,128)(2,1)S(1)}, bf16[256,2048]{1,0:T(8,128)(2,1)}, u32[]{:S(2)}) copy-start(bf16[256,2048]{1,0:T(8,128)(2,1)} %param.20) | copy-start | bytes 3145732
  38.6 1.9 copy-start.11
  64.9 2.7 copy-start.20
  64.9 2.7 copy-start.23
  78.1 9.1 %copy-start.9 = (bf16[1024,2048]{1,0:T(8,128)(2,1)S(1)}, bf16[1024,2048]{1,0:T(8,128)(2,1)}, u32[]{:S(2)}) copy-start(bf16[1024,2048]{1,0:T(8,128)(2,1)} %copy-done.8) | copy-start | bytes 12582916
  78.1 9.1 %copy-start.39 = (bf16[2048,1024]{1,0:T(8,128)(2,1)S(1)}, bf16[2048,1024]{1,0:T(8,128)(2,1)}, u32[]{:S(2)}) copy-start(bf16[2048,1024]{1,0:T(8,128)(2,1)} %param.22) | copy-start | bytes 12582916
  87.1 6.2 copy-start.37
  87.1 6.2 copy-start.38
  103.3 6.9 %copy-start.13 = (f32[1024,32]{0,1:T(8,128)S(1)}, f32[1024,32]{0,1:T(8,128)}, u32[]{:S(2)}) copy-start(f32[1024,32]{0,1:T(8,128)} %copy-done.12) | copy-start | bytes 393220
  110.2 0.9 copy-start.16
  110.5 1.1 copy-start.25
  111.4 2.8 copy-start.40
  111.4 3.5 copy-start.44
  112.0 7.4 %copy-start.14 = (bf16[1024,4,3,64]{0,3,2,1:T(8,128)(2,1)}, bf16[1024,4,3,64]{0,3,2,1:T(8,128)(2,1)S(1)}, u32[]{:S(2)}) copy-start(bf16[1024,4,3,64]{0,3,2,1:T(8,128)(2,1)S(1)} %copy.56) | copy-start | bytes 4718596
  119.4 5.4 copy-start.18
  119.4 5.4 copy-start.24
  128.1 277.3 %reduce-scatter.7.cloned.1.call-start = ((), (), s32[]{:S(2)}) async-start(), calls=%async_computation.5 | async-start | bytes 2228224 | tf_op jit(solution)/shard_map/reduce_scatter | solution.py:169
  133.3 283.7 %reduce-scatter.5.cloned.1.call-start = ((), (), s32[]{:S(2)}) async-start(), calls=%async_computation.4 | async-start | bytes 6684672 | tf_op jit(solution)/shard_map/reduce_scatter | solution.py:167
  142.2 380.4 %reduce-scatter.9.cloned.1.call-start = ((), (), s32[]{:S(2)}) async-start(), calls=%async_computation.6 | async-start | bytes 8912896 | tf_op jit(solution)/shard_map/reduce_scatter | solution.py:171
  153.1 475.4 %reduce-scatter.11.cloned.1.call-start = ((), (), s32[]{:S(2)}) async-start(), calls=%async_computation.7 | async-start | bytes 8912896 | tf_op jit(solution)/shard_map/reduce_scatter | solution.py:173
  166.1 0.7 copy-start.42
  166.1 3.2 copy-start.34
  166.1 3.2 copy-start.35
  166.1 149.5 %copy-start.27 = (f32[2048]{0:T(1024)S(1)}, f32[2048]{0:T(1024)}, u32[]{:S(2)}) copy-start(f32[2048]{0:T(1024)} %copy-done.26) | copy-start | bytes 24580
  166.1 149.5 %copy-start.29 = (f32[1024]{0:T(1024)S(1)}, f32[1024]{0:T(1024)}, u32[]{:S(2)}) copy-start(f32[1024]{0:T(1024)} %copy-done.28) | copy-start | bytes 12292
  166.1 149.5 %copy-start.31 = (f32[1024]{0:T(1024)S(1)}, f32[1024]{0:T(1024)}, u32[]{:S(2)}) copy-start(f32[1024]{0:T(1024)} %copy-done.30) | copy-start | bytes 12292
  315.6 6.4 %copy-start.3 = (bf16[1024,2048]{1,0:T(8,128)(2,1)S(1)}, bf16[1024,2048]{1,0:T(8,128)(2,1)}, u32[]{:S(2)}) copy-start(bf16[1024,2048]{1,0:T(8,128)(2,1)} %param.13) | copy-start | bytes 12582916
  315.6 6.4 %copy-start.4 = (bf16[1024,2048]{1,0:T(8,128)(2,1)S(1)}, bf16[1024,2048]{1,0:T(8,128)(2,1)}, u32[]{:S(2)}) copy-start(bf16[1024,2048]{1,0:T(8,128)(2,1)} %get-tuple-element.22) | copy-start | bytes 12582916
  403.1 225.8 %copy-start.43 = (f32[128]{0:T(128)}, f32[128]{0:T(128)S(1)}, u32[]{:S(2)}) copy-start(f32[128]{0:T(128)S(1)} %dynamic-slice.7) | copy-start | bytes 1540
Sparse Core Ops, SparseCore 0:
  128.2 187.2 all-reduce.16
Sparse Core Ops, SparseCore 1:
  133.3 193.0 reduce-scatter.6
  331.0 85.9 reduce-scatter.4
  421.7 100.8 reduce-scatter.8
  527.5 100.9 reduce-scatter.10
where the time goes:
time: 647 us; the launch traced here: 637 us
  waiting for transfers between devices  369 us (57%)
  matrix products  116 us (18%)
  blocking collectives  69.6 us (11%)
  other arithmetic  46.1 us (7%)
  between operations  18.8 us (3%)
  local copies, waits for them, and re-layouts  16.5 us (3%)
    psum x1, waiting for transfers between devices, per_device(): lax.psum((attn_part + mlp_part).astype(jnp.bfloat16), 'tensor')  146 us
    reduce_scatter x1, waiting for transfers between devices, per_device(): lax.psum_scatter(grad_fc2, 'dp', scatter_dimension=1, tiled=True)  106 us
    reduce_scatter x1, waiting for transfers between devices, per_device(): lax.psum_scatter(grad_fc1, 'dp', scatter_dimension=0, tiled=True)  106 us
    unnamed x1, blocking collectives  69.6 us
    unnamed x97, local copies, waits for them, and re-layouts  14.5 us
  transfers between devices with their start and end apart: 5, of which 4 were waited for; matrix products, arithmetic and copies ran while one was open for 9% of the time, Pallas kernels for 0%

commit v1 on v0

v1 whole, which is shorter than its diff:
```python
import functools

import jax
import jax.numpy as jnp
from jax import lax
from jax.experimental import pallas as pl
from jax.experimental.pallas import tpu as pltpu
from jax.sharding import Mesh
from jax.sharding import PartitionSpec as P

HEAD_DIM = 64
ROTARY = 32
DP = ("zh", "x", "core")
TENSOR = ("zl", "y")
BF16 = jnp.bfloat16
F32 = jnp.float32
ROWS = 256
BLOCK = 128
VMEM_BYTES = 56 * 2**20
GELU = 0.7978845608
SMALL_COST = pl.CostEstimate(flops=1, bytes_accessed=1, transcendentals=0)


def dot(left, right, left_dim, right_dim):
    return lax.dot_general(
        left, right, (((left_dim,), (right_dim,)), ((), ())), preferred_element_type=F32
    )


def kernel_call(kernel, name, out_shape, prefetch=0, **spec):
    if prefetch:
        spec = {
            "grid_spec": pltpu.PrefetchScalarGridSpec(
                num_scalar_prefetch=prefetch,
                grid=spec.pop("grid"),
                in_specs=spec.pop("in_specs"),
                out_specs=spec.pop("out_specs"),
                scratch_shapes=spec.pop("scratch_shapes", ()),
            ),
            **spec,
        }
    return pl.pallas_call(
        kernel,
        out_shape=out_shape,
        compiler_params=pltpu.CompilerParams(vmem_limit_bytes=VMEM_BYTES),
        cost_estimate=SMALL_COST,
        name=name,
        **spec,
    )


def made(rows, columns, kind=BF16):
    return jax.ShapeDtypeStruct((rows, columns), kind)


def kept(array):
    return pl.BlockSpec(array.shape, lambda *_: (0,) * array.ndim)


AWAY = pl.BlockSpec(memory_space=pl.ANY)
NEAR = pl.BlockSpec(memory_space=pltpu.VMEM)
SCALARS = pl.BlockSpec(memory_space=pltpu.SMEM)


def ends_of(lengths_ref):
    ends = []
    total = jnp.int32(0)
    for place in range(lengths_ref.shape[1]):
        total = total + lengths_ref[0, place]
        ends.append(total)
    return ends


def starts_at(ends, places):
    start = jnp.zeros_like(places)
    for end in ends:
        start = jnp.maximum(start, jnp.where(places >= end, end, 0))
    return start


def turned_halves(columns):
    lane = lax.broadcasted_iota(jnp.int32, columns.shape, 1)
    return jnp.where(
        lane % ROTARY < ROTARY // 2, pltpu.roll(columns, 112, 1), pltpu.roll(columns, 16, 1)
    )


def weight_copies(step, sources, targets, sems):
    copies = [
        pltpu.make_async_copy(source, target, sems.at[i])
        for i, (source, target) in enumerate(zip(sources, targets))
    ]

    @pl.when(step == 0)
    def _():
        for copy in copies:
            copy.start()

    def wait(i):
        @pl.when(step == 0)
        def _():
            copies[i].wait()

    return wait


def front_kernel(
    lengths_ref,
    freq_ref,
    tokens_ref,
    cot_ref,
    gain_ref,
    bias_ref,
    b_qkv_ref,
    b_fc1_ref,
    w_qkv_hbm,
    w_fc1_hbm,
    w_dense_hbm,
    hidden_ref,
    grad_ref,
    qkv_ref,
    act_ref,
    slope_ref,
    ctx_grad_ref,
    cos_ref,
    sin_ref,
    stats_ref,
    w_qkv,
    w_fc1,
    w_dense,
    sems,
):
    step = pl.program_id(0)
    wait = weight_copies(
        step, (w_qkv_hbm, w_fc1_hbm, w_dense_hbm), (w_qkv, w_fc1, w_dense), sems
    )
    rows = tokens_ref.shape[0]
    ends = ends_of(lengths_ref)
    places = step * rows + lax.broadcasted_iota(jnp.int32, (rows, 128), 0)
    position = (places - starts_at(ends, places)).astype(F32)
    lane = lax.broadcasted_iota(jnp.int32, (rows, 128), 1)
    angle = position * freq_ref[...]
    cosines = jnp.where(lane % HEAD_DIM < ROTARY, jnp.cos(angle), 1.0)
    sines = jnp.sin(angle)
    sines = jnp.where(
        lane % HEAD_DIM < ROTARY // 2, -sines, jnp.where(lane % HEAD_DIM < ROTARY, sines, 0.0)
    )
    cos_ref[...] = cosines
    sin_ref[...] = sines
    valid = (places < ends[-1])[:, :1]
    inputs = tokens_ref[...].astype(F32)
    mean = jnp.mean(inputs, axis=1, keepdims=True)
    center = inputs - mean
    inv_sigma = lax.rsqrt(jnp.mean(center * center, axis=1, keepdims=True) + 1e-05)
    stats_ref[...] = jnp.where(lane == 0, mean, inv_sigma)
    hidden = (
        center * inv_sigma * gain_ref[...].astype(F32)[None] + bias_ref[...].astype(F32)[None]
    ).astype(BF16)
    grad = jnp.where(valid, cot_ref[...], jnp.zeros_like(cot_ref))
    hidden_ref[...] = hidden
    grad_ref[...] = grad
    wait(0)
    projected = dot(hidden, w_qkv[...], 1, 0) + b_qkv_ref[...].astype(F32)[None]
    for block in range(qkv_ref.shape[1] // 128):
        columns = slice(block * 128, block * 128 + 128)
        plain = projected[:, columns]
        turned = plain * cosines + turned_halves(plain) * sines
        if block % 3 == 1:
            turned = jnp.where(lane < HEAD_DIM, plain, turned)
        if block % 3 == 2:
            turned = jnp.where(lane < HEAD_DIM, turned, plain)
        qkv_ref[:, columns] = turned.astype(BF16)
    wait(1)
    for block in range(w_fc1.shape[1] // 256):
        columns = slice(block * 256, block * 256 + 256)
        up = dot(hidden, w_fc1[:, columns], 1, 0) + b_fc1_ref[columns].astype(F32)[None]
        square = up * up
        tanh = jnp.tanh(GELU * up * (1.0 + 0.044715 * square))
        act_ref[:, columns] = (0.5 * up * (1.0 + tanh)).astype(BF16)
        slope_ref[:, columns] = (
            0.5 * (1.0 + tanh)
            + 0.5 * up * (1.0 - tanh * tanh) * (GELU + (GELU * 3 * 0.044715) * square)
        ).astype(BF16)
    wait(2)
    ctx_grad_ref[...] = dot(grad, w_dense[...], 1, 1).astype(BF16)


def front(lengths, freq, tokens, cot, gain, bias, b_qkv, b_fc1, w_qkv, w_fc1, w_dense):
    slot_len, width = tokens.shape

    def row(columns):
        return pl.BlockSpec((ROWS, columns), lambda i: (i, 0))

    widths = (width, width, w_qkv.shape[1], w_fc1.shape[1], w_fc1.shape[1], w_dense.shape[0])
    return kernel_call(
        front_kernel,
        "front",
        [made(slot_len, w) for w in widths] + [made(slot_len, 128, F32)] * 3,
        grid=(slot_len // ROWS,),
        in_specs=[SCALARS, kept(freq), row(width), row(width)]
        + [kept(a) for a in (gain, bias, b_qkv, b_fc1)]
        + [AWAY] * 3,
        out_specs=[row(w) for w in widths] + [row(128)] * 3,
        scratch_shapes=[
            pltpu.VMEM(w_qkv.shape, BF16),
            pltpu.VMEM(w_fc1.shape, BF16),
            pltpu.VMEM(w_dense.shape, BF16),
            pltpu.SemaphoreType.DMA((3,)),
        ],
    )(lengths, freq, tokens, cot, gain, bias, b_qkv, b_fc1, w_qkv, w_fc1, w_dense)


def attention_kernel(
    lengths_ref, qkv_ref, ctx_grad_ref, cos_ref, sin_ref, ctx_ref, qkv_grad_ref, turn_sum, value_sum
):
    slot_len = qkv_ref.shape[0]
    ends = ends_of(lengths_ref)
    for head in range(2):
        at = 3 * HEAD_DIM * head
        mine = slice(HEAD_DIM * head, HEAD_DIM * head + HEAD_DIM)
        for block in reversed(range(slot_len // ROWS)):
            rows = slice(block * ROWS, block * ROWS + ROWS)
            reach = (block + 1) * ROWS
            query = qkv_ref[rows, at : at + 64] * BF16(HEAD_DIM**-0.5)
            key = qkv_ref[0:reach, at + 64 : at + 128]
            value = qkv_ref[0:reach, at + 128 : at + 192]
            upstream = ctx_grad_ref[rows, mine]
            scores = dot(key, query, 1, 1)
            place = block * ROWS + lax.broadcasted_iota(jnp.int32, (1, ROWS), 1)
            start = starts_at(ends, place)
            key_place = lax.broadcasted_iota(jnp.int32, (reach, ROWS), 0)
            scores = jnp.where((key_place >= start) & (key_place <= place), scores, -1e30)
            raised = jnp.exp(scores - jnp.max(scores, axis=0, keepdims=True))
            prob = raised * (1.0 / jnp.sum(raised, axis=0, keepdims=True))
            prob_low = prob.astype(BF16)
            ctx = dot(value, prob_low, 0, 0)
            prob_grad = dot(value, upstream, 1, 1)
            row_dot = jnp.sum(prob_grad * prob, axis=0, keepdims=True)
            score_grad = (prob * (prob_grad - row_dot)).astype(BF16)
            query_grad = dot(key, score_grad, 0, 0)
            value_part = dot(prob_low, upstream, 1, 0)
            key_part = dot(score_grad, query, 1, 0)
            if reach == slot_len:
                value_sum[...] = value_part
                turn_sum[:, 64:128] = key_part
            else:
                value_sum[0:reach] += value_part
                turn_sum[0:reach, 64:128] += key_part
            turn_sum[rows, 0:64] = query_grad.T * HEAD_DIM**-0.5
            ctx_ref[rows, mine] = ctx.T.astype(BF16)
        both = turn_sum[...]
        both = both * cos_ref[...] - turned_halves(both) * sin_ref[...]
        qkv_grad_ref[:, at : at + 128] = both.astype(BF16)
        qkv_grad_ref[:, at + 128 : at + 192] = value_sum[...].astype(BF16)


def attention(lengths, qkv, ctx_grad, cosines, sines):
    slot_len = qkv.shape[0]
    pairs = qkv.shape[1] // 384

    def mine(columns):
        return pl.BlockSpec((slot_len, columns), lambda i: (0, i))

    return kernel_call(
        attention_kernel,
        "attention",
        [made(slot_len, 128 * pairs), made(slot_len, 384 * pairs)],
        grid=(pairs,),
        in_specs=[SCALARS, mine(384), mine(128), kept(cosines), kept(sines)],
        out_specs=[mine(128), mine(384)],
        scratch_shapes=[pltpu.VMEM((slot_len, 128), F32), pltpu.VMEM((slot_len, 64), F32)],
    )(lengths, qkv, ctx_grad, cosines, sines)


OFFSETS = tuple((planes, places) for planes in range(2) for places in range(4))
FAR = (1, 2)
CUTS = (0, 48, 96, 128)
PARTS = tuple(zip(CUTS, CUTS[1:]))
BLOCK_NAMES = tuple(o for o in OFFSETS if o != FAR) + (0, 1, 2)


def block_shapes(width):
    return [made(BLOCK, width)] * 7 + [made(high - low, width) for low, high in PARTS]


def block_specs(columns):
    heights = [BLOCK] * 7 + [high - low for low, high in PARTS]
    return [pl.BlockSpec((height, columns), lambda i, *_: (0, i)) for height in heights]


def store_blocks(places_ref, total, refs):
    def rows(offset, low, high):
        first = pl.multiple_of(places_ref[OFFSETS.index(offset)] * BLOCK, BLOCK)
        return total[pl.ds(first + low, high - low), :].astype(BF16)

    for name, ref in zip(BLOCK_NAMES, refs):
        if isinstance(name, int):
            ref[...] = rows(FAR, *PARTS[name])
        else:
            ref[...] = rows(name, 0, BLOCK)


def branch_kernel(ctx_ref, act_ref, w_dense_ref, w_fc2_ref, out_ref):
    out_ref[...] = (
        dot(ctx_ref[...], w_dense_ref[...], 1, 0) + dot(act_ref[...], w_fc2_ref[...], 1, 0)
    ).astype(BF16)


def branch(context, activated, w_dense, w_fc2):
    slot_len, width = context.shape[0], w_fc2.shape[1]

    def chunk(rows):
        return pl.BlockSpec((rows, 256), lambda i: (0, i))

    return kernel_call(
        branch_kernel,
        "branch",
        made(slot_len, width),
        grid=(width // 256,),
        in_specs=[
            kept(context),
            kept(activated),
            chunk(w_dense.shape[0]),
            chunk(w_fc2.shape[0]),
        ],
        out_specs=chunk(slot_len),
    )(context, activated, w_dense, w_fc2)


def units_kernel(grad_ref, w_fc2_ref, slope_ref, up_grad_ref, unit_sums_ref, grad_sums_ref):
    up_grad = (dot(grad_ref[...], w_fc2_ref[...], 1, 1) * slope_ref[...].astype(F32)).astype(BF16)
    up_grad_ref[...] = up_grad
    unit_sums_ref[...] = jnp.sum(up_grad.astype(F32), axis=0, keepdims=True)

    @pl.when(pl.program_id(0) == 0)
    def _():
        grad_sums_ref[...] = jnp.sum(grad_ref[...].astype(F32), axis=0, keepdims=True)


def units_back(grad, w_fc2, slope):
    slot_len, width = grad.shape
    units = w_fc2.shape[0]
    return kernel_call(
        units_kernel,
        "units",
        [made(slot_len, units), made(1, units, F32), made(1, width, F32)],
        grid=(units // 256,),
        in_specs=[
            kept(grad),
            pl.BlockSpec((256, width), lambda i: (i, 0)),
            pl.BlockSpec((slot_len, 256), lambda i: (0, i)),
        ],
        out_specs=[
            pl.BlockSpec((slot_len, 256), lambda i: (0, i)),
            pl.BlockSpec((1, 256), lambda i: (0, i)),
            pl.BlockSpec((1, width), lambda i: (0, 0)),
        ],
    )(grad, w_fc2, slope)


def hidden_kernel(
    places_ref,
    up_grad_ref,
    qkv_grad_ref,
    w_fc1_ref,
    w_qkv_ref,
    tokens_ref,
    stats_ref,
    gain_sum_ref,
    shift_sum_ref,
    head_sum_ref,
    *rest,
):
    *refs, total = rest
    part = dot(up_grad_ref[...], w_fc1_ref[...], 1, 1) + dot(
        qkv_grad_ref[...], w_qkv_ref[...], 1, 1
    )
    total[...] = part
    store_blocks(places_ref, total, refs)
    normed = (tokens_ref[...].astype(F32) - stats_ref[:, 0:1]) * stats_ref[:, 1:2]
    gain_sum_ref[...] = jnp.sum(part * normed, axis=0, keepdims=True)
    shift_sum_ref[...] = jnp.sum(part, axis=0, keepdims=True)

    @pl.when(pl.program_id(0) == 0)
    def _():
        head_sum_ref[...] = jnp.sum(qkv_grad_ref[...].astype(F32), axis=0, keepdims=True)


def hidden_blocks(places, up_grad, qkv_grad, w_fc1, w_qkv, tokens, stats):
    slot_len, width = tokens.shape

    def chunk(rows):
        return pl.BlockSpec((rows, 256), lambda i, *_: (0, i))

    gain_sum, shift_sum, head_sum, *blocks = kernel_call(
        hidden_kernel,
        "hidden",
        [made(1, width, F32), made(1, width, F32), made(1, qkv_grad.shape[1], F32)]
        + block_shapes(width),
        prefetch=1,
        grid=(width // 256,),
        in_specs=[
            kept(up_grad),
            kept(qkv_grad),
            pl.BlockSpec((256, w_fc1.shape[1]), lambda i, *_: (i, 0)),
            pl.BlockSpec((256, w_qkv.shape[1]), lambda i, *_: (i, 0)),
            chunk(slot_len),
            kept(stats),
        ],
        out_specs=[
            chunk(1),
            chunk(1),
            pl.BlockSpec((1, qkv_grad.shape[1]), lambda i, *_: (0, 0)),
        ]
        + block_specs(256),
        scratch_shapes=[pltpu.VMEM((slot_len, 256), F32)],
    )(places, up_grad, qkv_grad, w_fc1, w_qkv, tokens, stats)
    return gain_sum, shift_sum, head_sum, dict(zip(BLOCK_NAMES, blocks))


def weight_kernel(order_ref, left_a_ref, left_b_ref, first_ref, second_ref, *rest):
    *sums, out_ref = rest
    cut, end = first_ref.shape[1], first_ref.shape[1] + second_ref.shape[1]
    left = jnp.concatenate([left_a_ref[...], left_b_ref[...]], axis=1)
    out_ref[:, 0:cut] = dot(left, first_ref[...], 0, 0).astype(BF16)
    out_ref[:, cut:end] = dot(left, second_ref[...], 0, 0).astype(BF16)
    if sums:
        for half in range(2):
            block = order_ref[2 * pl.program_id(0) + half]
            lines = [ref[pl.ds(block, 1), :] for ref in sums]
            lines.append(jnp.zeros((BLOCK - len(lines), BLOCK), F32))
            columns = jnp.concatenate(lines, axis=0).T
            out_ref[half * BLOCK : half * BLOCK + BLOCK, end:] = columns.astype(BF16)


def weight_blocks(order, left, first, second, *sums):
    slot_len = left.shape[0]
    width = first.shape[1] + second.shape[1] + (BLOCK if sums else 0)
    return kernel_call(
        weight_kernel,
        "weights",
        made(left.shape[1], width),
        prefetch=1,
        grid=(left.shape[1] // (2 * BLOCK),),
        in_specs=[
            pl.BlockSpec((slot_len, BLOCK), lambda i, order: (0, order[2 * i])),
            pl.BlockSpec((slot_len, BLOCK), lambda i, order: (0, order[2 * i + 1])),
            kept(first),
            kept(second),
            *[kept(array) for array in sums],
        ],
        out_specs=pl.BlockSpec((2 * BLOCK, width), lambda i, order: (i, 0)),
    )(order, left, left, first, second, *sums)


def combine(name, *sums):
    arrays = [term[0] for terms in sums for term in terms]
    specs = [
        pl.BlockSpec((term[1], term[0].shape[1]), functools.partial(lambda at, _: (at, 0), term[2]))
        for terms in sums
        for term in terms
    ]
    heights = [max(term[4] for term in terms) for terms in sums]

    def kernel(*refs):
        ins, outs = list(refs[: len(arrays)]), refs[len(arrays) :]
        for terms, height, out in zip(sums, heights, outs):
            mine = [(ins.pop(0), term[3], term[4]) for term in terms]
            cuts = sorted({cut for _, low, high in mine for cut in (low, high)})
            for low, high in zip(cuts, cuts[1:]):
                parts = [
                    ref[low - first : high - first, :].astype(F32)
                    for ref, first, last in mine
                    if first <= low and high <= last
                ]
                out[low:high, :] = functools.reduce(lambda a, b: a + b, parts).astype(BF16)

    shapes = [made(height, terms[0][0].shape[1]) for height, terms in zip(heights, sums)]
    return kernel_call(
        kernel,
        name,
        shapes,
        grid=(1,),
        in_specs=specs,
        out_specs=[pl.BlockSpec(shape.shape, lambda _: (0, 0)) for shape in shapes],
    )(*arrays)


def whole_term(array, low=0):
    return (array, array.shape[0], 0, low, low + array.shape[0])


def output_kernel(lengths_ref, tokens_ref, branch_ref, b_dense_ref, b_fc2_ref, out_ref):
    bias = b_dense_ref[...].astype(F32) + b_fc2_ref[...].astype(F32)
    rows = tokens_ref.shape[0]
    place = pl.program_id(0) * rows + lax.broadcasted_iota(jnp.int32, (rows, 1), 0)
    total = jnp.where(
        place < ends_of(lengths_ref)[-1], branch_ref[...].astype(F32) + bias[None], 0.0
    )
    out_ref[...] = (tokens_ref[...].astype(F32) + total).astype(BF16)


def finish_output(lengths, tokens, branch_sum, b_dense, b_fc2):
    slot_len, width = tokens.shape
    row = pl.BlockSpec((ROWS, width), lambda i: (i, 0))
    return kernel_call(
        output_kernel,
        "output",
        made(slot_len, width),
        grid=(slot_len // ROWS,),
        in_specs=[SCALARS, row, row, kept(b_dense), kept(b_fc2)],
        out_specs=row,
    )(lengths, tokens, branch_sum, b_dense, b_fc2)


def input_kernel(places_ref, *refs):
    *terms, tokens_ref, cot_ref, stats_ref, gain_ref, out_ref = refs
    total = functools.reduce(lambda a, b: a + b, [t[...].astype(F32) for t in terms])
    inv_sigma = stats_ref[:, 1:2]
    normed = (tokens_ref[...].astype(F32) - stats_ref[:, 0:1]) * inv_sigma
    scaled = total * gain_ref[...].astype(F32)[None]
    out_ref[...] = (
        cot_ref[...].astype(F32)
        + inv_sigma
        * (
            scaled
            - jnp.mean(scaled, axis=1, keepdims=True)
            - normed * jnp.mean(scaled * normed, axis=1, keepdims=True)
        )
    ).astype(BF16)


def input_rows(places, terms, tokens, cot, stats, gain):
    width = tokens.shape[1]

    def mine(columns):
        return pl.BlockSpec((BLOCK, columns), lambda i, places: (places[0], 0))

    return kernel_call(
        input_kernel,
        "input",
        made(BLOCK, width),
        prefetch=1,
        grid=(1,),
        in_specs=[kept(t) for t in terms] + [mine(width), mine(width), mine(128), kept(gain)],
        out_specs=pl.BlockSpec((BLOCK, width), lambda *_: (0, 0)),
    )(places, *terms, tokens, cot, stats, gain)


def place_kernel(blocks, places_ref, *refs):
    pieces, out_ref, sems = refs[: len(blocks)], refs[-2], refs[-1]
    copies = []
    for i, ((offset, low, high), piece) in enumerate(zip(blocks, pieces)):
        first = pl.multiple_of(places_ref[OFFSETS.index(offset)] * BLOCK, BLOCK)
        copies.append(
            pltpu.make_async_copy(
                piece, out_ref.at[pl.ds(first + low, high - low), :], sems.at[i]
            )
        )
    for copy in copies:
        copy.start()
    for copy in copies:
        copy.wait()


def place_rows(places, blocks, pieces, whole=None):
    rest = {} if whole is None else {"input_output_aliases": {len(pieces) + 1: 0}}
    given = [] if whole is None else [whole]
    return kernel_call(
        functools.partial(place_kernel, blocks),
        "place",
        made(8 * BLOCK, pieces[0].shape[1]),
        in_specs=[SCALARS] + [NEAR] * len(pieces) + [AWAY] * len(given),
        out_specs=AWAY,
        scratch_shapes=[pltpu.SemaphoreType.DMA((len(pieces),))],
        **rest,
    )(places, *pieces, *given)


def up_kernel(near_ref, far_ref, first_ref, second_ref, sums_ref):
    total = near_ref[...].astype(F32) + far_ref[...].astype(F32)
    cut, end = first_ref.shape[1], first_ref.shape[1] + second_ref.shape[1]
    first_ref[...] = total[:, :cut]
    second_ref[...] = total[:, cut:end]
    sums_ref[...] = total[:, end:].T[: sums_ref.shape[0]]


def down_kernel(near_ref, far_ref, first_ref, second_ref):
    total = near_ref[...].astype(F32) + far_ref[...].astype(F32)
    cut = first_ref.shape[0]
    first_ref[...] = total[:, :cut].T
    second_ref[...] = total[:, cut:].T


def last_sum(kernel, name, shapes, near, far):
    return kernel_call(
        kernel,
        name,
        [made(*shape, F32) for shape in shapes],
        grid=(1,),
        in_specs=[pl.BlockSpec(far.shape, lambda _: (0, 0))] * 2,
        out_specs=[pl.BlockSpec(shape, lambda _: (0, 0)) for shape in shapes],
    )(near, far)


def shift(array, axis, size, by):
    return lax.ppermute(array, axis, [(i, (i + by) % size) for i in range(size)])


def y_up(array):
    return shift(array, "y", 4, 1)


def y_down(array):
    return shift(array, "y", 4, 3)


def across(array):
    return shift(array, "zl", 2, 1)


def after(arrays, *earlier):
    return lax.optimization_barrier((arrays, earlier))[0]


class TensorSum:
    def __init__(self, blocks):
        self.blocks = blocks

    def send_far(self, earlier):
        b = self.blocks
        sent = after([b[0], b[1], b[2], b[(0, 3)]], earlier)
        self.far = across(sent[0]), y_up(sent[1]), y_down(sent[2])
        self.near = [y_down(sent[3])]
        return sent

    def send_middle(self, earlier):
        b = self.blocks
        far = after(self.far, earlier)
        sent = combine(
            "middle",
            *[
                [whole_term(b[offset]), whole_term(part, low)]
                for offset, part, (low, _) in zip(((0, 2), (1, 1), (1, 3)), far, PARTS)
            ],
        )
        self.middle = y_up(sent[0]), across(sent[1]), y_down(sent[2])
        return sent

    def send_near(self, earlier):
        b = self.blocks
        two_on, diagonal, other = after(self.middle, earlier)
        sent = combine(
            "near",
            [whole_term(b[(0, 1)]), whole_term(two_on), whole_term(diagonal)],
            [whole_term(b[(1, 0)]), whole_term(other)],
        )
        self.near += [y_up(sent[0]), across(sent[1])]
        return sent

    def terms(self, earlier):
        return after([self.blocks[(0, 0)], *self.near], earlier)


class TensorGather:
    def __init__(self, places, rows):
        self.places, self.rows = places, rows
        self.one = y_up(rows), y_down(rows), across(rows)

    def second(self, earlier):
        before, ahead, partner = self.one = after(self.one, earlier)
        self.two = y_down(ahead), across(ahead), y_up(partner)
        return self.one

    def third(self, earlier):
        two_on, diagonal, other = self.two = after(self.two, earlier)
        (a, b), (c, d), (e, f) = PARTS
        self.three = across(two_on[a:b]), y_down(diagonal[c:d]), y_up(other[e:f])
        blocks = [(0, 0), (0, 3), (0, 1), (1, 0), (0, 2), (1, 1), (1, 3)]
        self.whole = place_rows(
            self.places,
            [(offset, 0, BLOCK) for offset in blocks],
            [self.rows, *self.one, *self.two],
        )
        return self.whole

    def finish(self, earlier):
        parts = after(self.three, earlier)
        return place_rows(
            self.places, [(FAR, low, high) for low, high in PARTS], list(parts), self.whole
        )


class DataSum:
    def __init__(self, partial_sums, earlier):
        self.near = lax.psum_scatter(
            after(partial_sums, earlier), ("x", "core"), scatter_dimension=0, tiled=True
        )

    def send(self, earlier):
        self.near = after(self.near, earlier)
        self.far = shift(self.near[BLOCK:], "zh", 2, 1)

    def finish(self, kernel, name, shapes, earlier):
        near, far = after([self.near, self.far], earlier)
        return last_sum(kernel, name, shapes, near, far)


def dp_order():
    half = lax.axis_index("zh")
    return jnp.stack(
        [(half + part) % 2 * 8 + block for block in range(8) for part in range(2)]
    ).astype(jnp.int32)


def per_device(
    tokens,
    cotangent,
    seq_lengths,
    ln_gain,
    ln_bias,
    w_qkv,
    b_qkv,
    w_dense,
    b_dense,
    w_fc1,
    b_fc1,
    w_fc2,
    b_fc2,
):
    units = w_fc2.shape[0]
    plane, place = lax.axis_index("zl"), lax.axis_index("y")
    places = jnp.stack(
        [(plane + planes) % 2 * 4 + (place + steps) % 4 for planes, steps in OFFSETS]
    ).astype(jnp.int32)
    order = dp_order()
    frequency = 10000.0 ** (-jnp.arange(ROTARY // 2, dtype=F32) * 2.0 / ROTARY)
    frequency = jnp.tile(frequency, 8)[None]
    hidden, grad, qkv, activated, slope, ctx_grad, cosines, sines, stats = front(
        seq_lengths,
        frequency,
        tokens,
        cotangent,
        ln_gain,
        ln_bias,
        b_qkv,
        b_fc1,
        w_qkv,
        w_fc1,
        w_dense,
    )
    context, qkv_grad = attention(seq_lengths, qkv, ctx_grad, cosines, sines)
    branch_part = branch(context, activated, w_dense, w_fc2)
    branch_sum = lax.psum(branch_part, TENSOR)
    up_grad, unit_sum, grad_sum = units_back(*after((grad, w_fc2, slope), branch_part))
    gain_sum, shift_sum, head_sum, blocks = hidden_blocks(
        places, up_grad, qkv_grad, w_fc1, w_qkv, tokens, stats
    )
    backward = TensorSum(blocks)
    sums = [
        gain_sum.reshape(16, -1),
        shift_sum.reshape(16, -1),
        grad_sum.reshape(16, -1),
        jnp.pad(head_sum.reshape(16, -1), ((0, 0), (0, 80))),
        jnp.pad(unit_sum.reshape(16, -1), ((0, 0), (0, 64))),
    ]
    done = backward.send_far(())
    up_part = weight_blocks(order, *after((hidden, up_grad, qkv_grad, *sums), done))
    done = backward.send_middle(up_part)
    up = DataSum(up_part, done)
    down_part = weight_blocks(order, *after((grad, activated, context), done))
    done = backward.send_near(down_part)
    down = DataSum(down_part, done)
    in_rows = input_rows(places, backward.terms((down_part, branch_sum)), tokens, cotangent, stats, ln_gain)
    input_grad = TensorGather(places, in_rows)
    up.send(in_rows)
    output = finish_output(seq_lengths, tokens, after(branch_sum, up.near), b_dense, b_fc2)
    done = input_grad.second(output)
    down.send(done)
    grad_fc1, grad_qkv, small = up.finish(
        up_kernel,
        "up",
        ((BLOCK, units), (BLOCK, w_qkv.shape[1]), (8, BLOCK)),
        down.near,
    )
    norm_sum = lax.psum(small[:2], TENSOR)
    input_grad.third(norm_sum)
    grad_fc2, grad_dense = down.finish(
        down_kernel, "down", ((units, BLOCK), (w_dense.shape[0], BLOCK)), input_grad.whole
    )
    input_grad = input_grad.finish(grad_dense)
    out_bias = small[2]
    return (
        output,
        input_grad,
        norm_sum[0],
        norm_sum[1],
        grad_qkv,
        small[3, :48],
        grad_dense,
        out_bias,
        grad_fc1,
        small[4, :64],
        grad_fc2,
        out_bias,
    )


def solution(mesh):
    parts = Mesh(mesh.devices.reshape(2, 4, 2, 2, 4), DP + TENSOR)
    rows = P(DP, None)
    placed = (
        rows,
        rows,
        rows,
        P(),
        P(),
        P(None, TENSOR),
        P(TENSOR),
        P(TENSOR, None),
        P(),
        P(None, TENSOR),
        P(TENSOR),
        P(TENSOR, None),
        P(),
    )
    return jax.shard_map(
        per_device,
        mesh=parts,
        in_specs=placed,
        out_specs=(
            rows,
            rows,
            P(DP),
            P(DP),
            P(DP, TENSOR),
            P(TENSOR + DP),
            P(TENSOR, DP),
            P(DP),
            P(DP, TENSOR),
            P(TENSOR + DP),
            P(TENSOR, DP),
            P(DP),
        ),
        check_vma=False,
    )
```

time: 647 us -> 277 us (0.43); the launches traced: 637 us -> 275 us
  waiting for transfers between devices: 369 us -> 46.5 us
  Pallas kernels: 0 us -> 140 us
  matrix products: 116 us -> 0 us
  blocking collectives: 69.6 us -> 18.9 us
  other arithmetic: 46.1 us -> 1.26 us
  starting transfers between devices: 0.47 us -> 38.2 us
    reduce_scatter x4 -> x2, waiting for transfers between devices: 223 us -> 0.01 us  [__init__(): lax.psum_scatter(after(partial_sums, earlier), ('x', 'core'), scatter_dim...]
    pallas_call x0 -> x15, Pallas kernels: none -> 140 us  [the longest x1 26.6 us: front(): kernel_call(front_kernel, 'front', [made(slot_len, w) for w in widths] +...]
    psum x1, waiting for transfers between devices: 146 us -> 8.33 us  [per_device(): branch_sum = lax.psum(branch_part, TENSOR)]
    dot_general x18 -> x0, matrix products: 116 us -> none  [the longest x1 12.7 us: per_device(): jnp.einsum('tf,td->fd', activated, branch_grad, preferred_element_type=jn...]
    unnamed x1 -> x0, blocking collectives: 69.6 us -> none
    ppermute x0 -> x20, waiting for transfers between devices: none -> 38.1 us  [shift(): lax.ppermute(array, axis, [(i, (i + by) % size) for i in range(size)])]
    ppermute x0 -> x20, starting transfers between devices: none -> 38.1 us  [shift(): lax.ppermute(array, axis, [(i, (i + by) % size) for i in range(size)])]
    reduce_sum x8 -> x0, other arithmetic: 26.1 us -> none  [the longest x1 11.5 us: per_device(): bias_grad = jnp.sum(branch_grad.astype(jnp.float32), axis=0)]
  transfers between devices with their start and end apart: 5 -> 23, of which waited for: 4 -> 9; matrix products, arithmetic and copies ran while one was open for 9% -> 4% of each run, Pallas kernels for 0% -> 28%
where the time goes in v1:
time: 277 us; the launch traced here: 275 us
  Pallas kernels  140 us (51%)
  waiting for transfers between devices  46.5 us (17%)
  starting transfers between devices  38.2 us (14%)
  blocking collectives  18.9 us (7%)
  between operations  15.8 us (6%)
  local copies, waits for them, and re-layouts  14.4 us (5%)
    ppermute x20, waiting for transfers between devices, shift(): lax.ppermute(array, axis, [(i, (i + by) % size) for i in range(size)])  38.1 us
    ppermute x20, starting transfers between devices, shift(): lax.ppermute(array, axis, [(i, (i + by) % size) for i in range(size)])  38.1 us
    pallas_call x1, Pallas kernels, front(): kernel_call(front_kernel, 'front', [made(slot_len, w) for w in widths] +...  26.6 us
    pallas_call x2, Pallas kernels, weight_blocks(): kernel_call(weight_kernel, 'weights', made(left.shape[1], width), prefetc...  26.2 us
    pallas_call x1, Pallas kernels, attention(): kernel_call(attention_kernel, 'attention', [made(slot_len, 128 * pairs),...  24 us
    psum x1, blocking collectives, per_device(): norm_sum = lax.psum(small[:2], TENSOR)  18.9 us
    pallas_call x1, Pallas kernels, hidden_blocks(): kernel_call(hidden_kernel, 'hidden', [made(1, width, F32), made(1, width,...  15.5 us
    pallas_call x1, Pallas kernels, branch(): kernel_call(branch_kernel, 'branch', made(slot_len, width), grid=(width /...  11.1 us
  transfers between devices with their start and end apart: 23, of which 9 were waited for; matrix products, arithmetic and copies ran while one was open for 4% of the time, Pallas kernels for 28%

profile of v1, /device:TPU:0, one launch (start us, length us, event | category | flops | bytes accessed | tf_op | source)
XLA Modules:
  0.0 275.2 jit_solution(17622727059670340455)
XLA Ops:
  8.1 0.6 broadcast_in_dim_tile.3.freq_ref
  8.7 26.6 %front.1 = (bf16[1024,2048]{1,0:T(8,128)(2,1)}, bf16[1024,2048]{1,0:T(8,128)(2,1)}, bf16[1024,768]{1,0:T(8,128)(2,1)}, bf16[1024,1024]{1,0:T(8,128)(2,1)}, bf16[...) custom-call(s32[1,8]{1,0:T(1,128)} %lengths_ref.5, ...), custom_call_target="tpu_custom_call" | custom-call | flops 1 | bytes 1 | tf_op jit(solution)/shard_map/front/pallas_call | solution.py:195
  35.2 24.0 %attention.1 = (bf16[1024,256]{1,0:T(8,128)(2,1)}, bf16[1024,768]{1,0:T(8,128)(2,1)}) custom-call(s32[1,8]{1,0:T(1,128)} %lengths_ref.5, bf16[1024,768]{1,0:T(8,128)(2,1)} %get-tuple-element.95.qkv_ref, bf16[1024,256]{1,0:T(8,128)(2,1)} %get-tuple-element.96.ctx_grad_ref, f32[1024,128]{1,0:T(8,128)} %get-tuple-element.97.cos_ref, ...), custom_call_target="tpu_custom_call" | custom-call | flops 1 | bytes 1 | tf_op jit(solution)/shard_map/attention/pallas_call | solution.py:264
  59.2 11.1 %branch.1 = bf16[1024,2048]{1,0:T(8,128)(2,1)} custom-call(bf16[1024,256]{1,0:T(8,128)(2,1)} %get-tuple-element.145.ctx_ref.second_ref, bf16[1024,1024]{1,0:T(8,128)(2,1)} %get-tuple-element.144.act_ref.first_ref, bf16[256,2048]{1,0:T(8,128)(2,1)} %w_dense_ref.1, bf16[1024,2048]{1,0:T(8,128)(2,1)} %w_fc2_ref.2), custom_call_target="tpu_custom_call" | custom-call | flops 1 | bytes 1 | tf_op jit(solution)/shard_map/branch/pallas_call | solution.py:315
  70.4 10.2 %units.1 = (bf16[1024,1024]{1,0:T(8,128)(2,1)}, f32[1,1024]{1,0:T(1,128)}, f32[1,2048]{1,0:T(1,128)}) custom-call(bf16[1024,2048]{1,0:T(8,128)(2,1)} %get-tuple-element.143.grad_ref.left_a_ref.left_b_ref, bf16[1024,2048]{1,0:T(8,128)(2,1)} %w_fc2_ref.2, bf16[1024,1024]{1,0:T(8,128)(2,1)} %get-tuple-element.106.slope_ref), custom_call_target="tpu_custom_call" | custom-call | flops 1 | bytes 1 | tf_op jit(solution)/shard_map/units/pallas_call | solution.py:343
  80.6 0.7 stack.103.places_ref
  81.3 15.5 %hidden.1 = (f32[1,2048]{1,0:T(1,128)}, f32[1,2048]{1,0:T(1,128)}, f32[1,768]{1,0:T(1,128)}, bf16[128,2048]{1,0:T(8,128)(2,1)}, bf16[128,2048]{1,0:T(8,128)(2,1)...) custom-call(s32[8]{0:T(128)} %stack.103.places_ref, ...), custom_call_target="tpu_custom_call" | custom-call | flops 1 | bytes 1 | tf_op jit(solution)/shard_map/hidden/pallas_call | solution.py:395
  96.8 2.1 collective-permute-start
  98.9 1.6 collective-permute-start.1
  100.5 1.7 collective-permute-start.2
  102.1 0.5 broadcast.34
  102.6 0.6 reduce.4
  103.3 0.7 reduce
  104.0 0.1 reshape.48
  104.1 0.6 pad.9.rest_4_
  104.7 0.6 pad.8.rest_3_
  105.3 0.6 stack.94.order_ref
  105.9 14.2 %weights.2 = bf16[2048,1920]{1,0:T(8,128)(2,1)} custom-call(s32[16]{0:T(128)} %stack.94.order_ref, bf16[1024,2048]{1,0:T(8,128)(2,1)} %get-tuple-element.123.left_a_ref.left_b_ref, bf16[1024,2048]{1,0:T(8,128)(2,1)} %get-tuple-element.123.left_a_ref.left_b_ref, bf16[1024,1024]{1,0:T(8,128)(2,1)} %get-tuple-element.124.up_grad_ref.first_ref, ...), custom_call_target="tpu_custom_call" | custom-call | flops 1 | bytes 1 | tf_op jit(solution)/shard_map/weights/pallas_call | solution.py:439
  120.1 0.6 copy-done.17
  120.8 2.8 %middle.1 = (bf16[128,2048]{1,0:T(8,128)(2,1)}, bf16[128,2048]{1,0:T(8,128)(2,1)}, bf16[128,2048]{1,0:T(8,128)(2,1)}) custom-call(bf16[128,2048]{1,0:T(8,128)(2,1)} %get-tuple-element.131.refs_0_, bf16[48,2048]{1,0:T(8,128)(2,1)} %copy-done.12, bf16[128,2048]{1,0:T(8,128)(2,1)} %get-tuple-element.133.refs_2_, bf16[48,2048]{1,0:T(8,128)(2,1)} %copy-done.13, ...), custom_call_target="tpu_custom_call" | custom-call | flops 1 | bytes 1 | tf_op jit(solution)/shard_map/middle/pallas_call | solution.py:479
  123.7 0.5 collective-permute-start.4
  124.2 0.5 copy-done.21
  124.7 0.1 collective-permute-start.5
  124.8 10.9 %collective-permute-start.6 = (bf16[128,2048]{1,0:T(8,128)(2,1)S(1)}, bf16[128,2048]{1,0:T(8,128)(2,1)S(1)}, u32[]{:S(2)}, u32[]{:S(2)}) collective-permute-start(bf16[128,2048]{1,0:T(8,128)(2,1)S(1)} %copy-done.20), channel_id=1, source_target_pairs={{0,3},{1,0},{2,1},{3,2},{4,7},{5,4},{6,5},{7,6},{8,11},{9,8},{10,9... | collective-permute-start | bytes 1572872 | tf_op jit(solution)/shard_map/ppermute | solution.py:607
  135.7 12.0 %weights.3 = bf16[2048,1280]{1,0:T(8,128)(2,1)} custom-call(s32[16]{0:T(128)} %stack.94.order_ref, bf16[1024,2048]{1,0:T(8,128)(2,1)} %get-tuple-element.143.grad_ref.left_a_ref.left_b_ref, bf16[1024,2048]{1,0:T(8,128)(2,1)} %get-tuple-element.143.grad_ref.left_a_ref.left_b_ref, bf16[1024,1024]{1,0:T(8,128)(2,1)} %get-tuple-element.144.act_ref.first_ref, ...), custom_call_target="tpu_custom_call" | custom-call | flops 1 | bytes 1 | tf_op jit(solution)/shard_map/weights/pallas_call | solution.py:439
  147.7 1.6 collective-permute-done.4.refs_1_
  149.3 5.2 %collective-permute-done.6.refs_4_ = bf16[128,2048]{1,0:T(8,128)(2,1)S(1)} collective-permute-done((bf16[128,2048]{1,0:T(8,128)(2,1)S(1)}, bf16[128,2048]{1,0:T(8,128)(2,1)S(1)}, u32[]{:S(2)}, u32[]{:S(2)}) %collective-permute-start.6) | collective-permute-done | bytes 524320 | tf_op jit(solution)/shard_map/ppermute | solution.py:607
  154.5 0.8 copy-done.8
  155.3 3.0 %near.1 = (bf16[128,2048]{1,0:T(8,128)(2,1)}, bf16[128,2048]{1,0:T(8,128)(2,1)}) custom-call(bf16[128,2048]{1,0:T(8,128)(2,1)} %get-tuple-element.142.refs_0_, bf16[128,2048]{1,0:T(8,128)(2,1)} %copy-done.6, bf16[128,2048]{1,0:T(8,128)(2,1)} %copy-done.7, bf16[128,2048]{1,0:T(8,128)(2,1)} %get-tuple-element.148.refs_3_, bf16[128,2048]{1,0:T(8,128)(2,1)} %copy-done.8), custom_call_target="tpu_custom_call" | custom-call | flops 1 | bytes 1 | tf_op jit(solution)/shard_map/near/pallas_call | solution.py:479
  158.3 3.8 %collective-permute-start.3 = (bf16[128,2048]{1,0:T(8,128)(2,1)S(1)}, bf16[128,2048]{1,0:T(8,128)(2,1)S(1)}, u32[]{:S(2)}, u32[]{:S(2)}) collective-permute-start(bf16[128,2048]{1,0:T(8,128)(2,1)S(1)} %copy-done.19), channel_id=1, source_target_pairs={{0,3},{1,0},{2,1},{3,2},{4,7},{5,4},{6,5},{7,6},{8,11},{9,8},{10,9... | collective-permute-start | bytes 1572872 | tf_op jit(solution)/shard_map/ppermute | solution.py:607
  162.1 0.5 collective-permute-start.8
  162.6 20.5 %collective-permute-done.3.refs_1_ = bf16[128,2048]{1,0:T(8,128)(2,1)S(1)} collective-permute-done((bf16[128,2048]{1,0:T(8,128)(2,1)S(1)}, bf16[128,2048]{1,0:T(8,128)(2,1)S(1)}, u32[]{:S(2)}, u32[]{:S(2)}) %collective-permute-start.3) | collective-permute-done | bytes 524320 | tf_op jit(solution)/shard_map/ppermute | solution.py:607
  183.1 3.5 %collective-permute-done.7.refs_2_ = bf16[128,2048]{1,0:T(8,128)(2,1)S(1)} collective-permute-done((bf16[128,2048]{1,0:T(8,128)(2,1)S(1)}, bf16[128,2048]{1,0:T(8,128)(2,1)S(1)}, u32[]{:S(2)}, u32[]{:S(2)}) %collective-permute-start.7) | collective-permute-done | bytes 524320 | tf_op jit(solution)/shard_map/ppermute | solution.py:607
  186.7 2.3 collective-permute-done.8.refs_3_
  188.9 8.3 %all-reduce.4.cloned.1.call-done.branch_ref = bf16[1024,2048]{1,0:T(8,128)(2,1)} async-done(((bf16[1024,2048]{1,0:T(8,128)(2,1)}), bf16[1024,2048]{1,0:T(8,128)(2,1)}) %all-reduce.4.cloned.1.call-update) | async-done | bytes 4194320 | tf_op jit(solution)/shard_map/psum | solution.py:754
  197.3 4.2 %input.1.refs_0_ = bf16[128,2048]{1,0:T(8,128)(2,1)} custom-call(s32[8]{0:T(128)} %stack.103.places_ref, bf16[128,2048]{1,0:T(8,128)(2,1)} %get-tuple-element.152.refs_0_, bf16[128,2048]{1,0:T(8,128)(2,1)} %copy-done.9, bf16[128,2048]{1,0:T(8,128)(2,1)} %copy-done.10, bf16[128,2048]{1,0:T(8,128)(2,1)} %copy-done.11, bf16[1024,2048]{1,0:T(8,128)(2,1)} %tokens_ref.5, ...), custom_call_target="tpu_custom_call" | custom-call | flops 1 | bytes 1 | tf_op jit(solution)/shard_map/input/pallas_call | solution.py:539
  201.5 1.9 collective-permute-start.11
  203.4 4.3 %collective-permute-start.10 = (bf16[128,2048]{1,0:T(8,128)(2,1)}, bf16[128,2048]{1,0:T(8,128)(2,1)S(1)}, u32[]{:S(2)}, u32[]{:S(2)}) collective-permute-start(bf16[128,2048]{1,0:T(8,128)(2,1)} %input.1.refs_0_), channel_id=1, source_target_pairs={{0,3},{1,0},{2,1},{3,2},{4,7},{5,4},{6,5},{7,6},{8,11},{9,8},{10,9... | collective-permute-start | bytes 1572872 | tf_op jit(solution)/shard_map/ppermute | solution.py:607
  207.7 1.9 slice.33
  209.5 6.5 %output.1 = bf16[1024,2048]{1,0:T(8,128)(2,1)} custom-call(s32[1,8]{1,0:T(1,128)} %lengths_ref.5, bf16[1024,2048]{1,0:T(8,128)(2,1)} %tokens_ref.5, bf16[1024,2048]{1,0:T(8,128)(2,1)} %all-reduce.4.cloned.1.call-done.branch_ref, bf16[2048]{0:T(1024)(128)(2,1)} %b_dense_ref.1, bf16[2048]{0:T(1024)(128)(2,1)} %b_fc2_ref.1), custom_call_target="tpu_custom_call" | custom-call | flops 1 | bytes 1 | tf_op jit(solution)/shard_map/output/pallas_call | solution.py:506
  216.0 0.5 collective-permute-done.11.refs_3_
  216.5 1.2 collective-permute-done.10.refs_2_
  217.7 3.3 %collective-permute-done.9.refs_1_ = bf16[128,2048]{1,0:T(8,128)(2,1)S(1)} collective-permute-done((bf16[128,2048]{1,0:T(8,128)(2,1)}, bf16[128,2048]{1,0:T(8,128)(2,1)S(1)}, u32[]{:S(2)}, u32[]{:S(2)}) %collective-permute-start.9) | collective-permute-done | bytes 524320 | tf_op jit(solution)/shard_map/ppermute | solution.py:607
  221.1 1.6 collective-permute-start.13
  222.6 0.6 collective-permute-start.12
  223.3 1.4 collective-permute-start.14
  224.7 1.0 slice.38
  225.7 2.4 collective-permute-start.19
  228.1 2.2 up.1
  230.2 0.7 slice_bitcast_fusion.1
  230.9 1.2 slice_bitcast_fusion
  232.1 1.2 slice_bitcast_fusion.2
  233.3 0.7 slice.34
  234.0 18.9 %psum.15 = f32[2,128]{1,0:T(2,128)S(1)} all-reduce(f32[2,128]{1,0:T(2,128)S(1)} %slice.34), channel_id=1, replica_groups=mesh['zh'=2,'x'=4,'core'=2,'zl'=2,'y'=4] {'zl','y'}, use_global_device_ids=true, to_apply=%region_3.4 | all-reduce | flops 256 | bytes 2048 | tf_op jit(solution)/shard_map/psum | solution.py:786
  253.0 0.1 collective-permute-start.18
  253.1 3.3 %collective-permute-start.17 = (bf16[48,2048]{1,0:T(8,128)(2,1)S(1)}, bf16[48,2048]{1,0:T(8,128)(2,1)S(1)}, u32[]{:S(2)}, u32[]{:S(2)}) collective-permute-start(bf16[48,2048]{1,0:T(8,128)(2,1)S(1)} %slice.36), channel_id=1, source_target_pairs={{0,3},{1,0},{2,1},{3,2},{4,7},{5,4},{6,5},{7,6},{8,11},{9,8},{10,9... | collective-permute-start | bytes 589832 | tf_op jit(solution)/shard_map/ppermute | solution.py:607
  256.4 1.5 collective-permute-start.16
  257.9 0.5 slice_bitcast_fusion.3
  258.5 3.9 %place.2.refs_3_ = bf16[1024,2048]{1,0:T(8,128)(2,1)} custom-call(s32[8]{0:T(128)} %stack.103.places_ref, bf16[128,2048]{1,0:T(8,128)(2,1)} %input.1.refs_0_, bf16[128,2048]{1,0:T(8,128)(2,1)} %copy-done.5, bf16[128,2048]{1,0:T(8,128)(2,1)} %copy-done.4, bf16[128,2048]{1,0:T(8,128)(2,1)} %copy-done.3, bf16[128,2048]{1,0:T(8,128)(2,1)} %copy-done.1, ...), custom_call_target="tpu_custom_call" | custom-call | flops 1 | bytes 1 | tf_op jit(solution)/shard_map/place/pallas_call | solution.py:569
  262.4 2.1 down.1
  264.6 0.6 copy-done.16
  265.2 0.1 copy-done.14
  265.3 1.9 place.3
  267.2 0.5 copy.29
  (74 shorter events, 0.7 us)
Async XLA Ops:
  8.0 189.3 %all-reduce.4.cloned.1.call-start = ((), (), s32[]{:S(2)}) async-start(), calls=%async_computation.2 | async-start | bytes 8388608 | tf_op jit(solution)/shard_map/psum | solution.py:754
  70.4 137.3 %reduce-scatter.3.cloned.1.call-start = ((), (), s32[]{:S(2)}) async-start(), calls=%async_computation.3 | async-start | bytes 8847360 | tf_op jit(solution)/shard_map/reduce_scatter | solution.py:696
  81.3 21.3 %copy-start.18 = (f32[1,1024]{1,0:T(1,128)S(1)}, f32[1,1024]{1,0:T(1,128)}, u32[]{:S(2)}) copy-start(f32[1,1024]{1,0:T(1,128)} %get-tuple-element.114) | copy-start | bytes 12292
  96.8 23.3 %collective-permute-start = (bf16[48,2048]{1,0:T(8,128)(2,1)}, bf16[48,2048]{1,0:T(8,128)(2,1)S(1)}, u32[]{:S(2)}, u32[]{:S(2)}) collective-permute-start(bf16[48,2048]{1,0:T(8,128)(2,1)} %get-tuple-element.119), channel_id=1, source_target_pairs={{0,4},{4,0},{1,5},{5,1},{2,6},{6,2},{3,7},{7,3},{8,12},{12,8},{9,1... | collective-permute-start | bytes 589832 | tf_op jit(solution)/shard_map/ppermute | solution.py:607
  98.9 21.2 %collective-permute-start.1 = (bf16[48,2048]{1,0:T(8,128)(2,1)}, bf16[48,2048]{1,0:T(8,128)(2,1)S(1)}, u32[]{:S(2)}, u32[]{:S(2)}) collective-permute-start(bf16[48,2048]{1,0:T(8,128)(2,1)} %get-tuple-element.120), channel_id=1, source_target_pairs={{0,1},{1,2},{2,3},{3,0},{4,5},{5,6},{6,7},{7,4},{8,9},{9,10},{10,1... | collective-permute-start | bytes 589832 | tf_op jit(solution)/shard_map/ppermute | solution.py:607
  100.5 19.6 %collective-permute-start.2 = (bf16[32,2048]{1,0:T(8,128)(2,1)}, bf16[32,2048]{1,0:T(8,128)(2,1)S(1)}, u32[]{:S(2)}, u32[]{:S(2)}) collective-permute-start(bf16[32,2048]{1,0:T(8,128)(2,1)} %get-tuple-element.121), channel_id=1, source_target_pairs={{0,3},{1,0},{2,1},{3,2},{4,7},{5,4},{6,5},{7,6},{8,11},{9,8},{10,9... | collective-permute-start | bytes 393224 | tf_op jit(solution)/shard_map/ppermute | solution.py:607
  120.1 0.7 copy-start.17
  120.1 0.7 copy-start.12
  120.1 0.7 copy-start.13
  123.6 1.0 copy-start.21
  123.6 1.2 copy-start.20
  123.7 101.0 %reduce-scatter.5.cloned.1.call-start = ((), (), s32[]{:S(2)}) async-start(), calls=%async_computation.4 | async-start | bytes 5898240 | tf_op jit(solution)/shard_map/reduce_scatter | solution.py:696
  123.7 25.6 %collective-permute-start.4 = (bf16[128,2048]{1,0:T(8,128)(2,1)}, bf16[128,2048]{1,0:T(8,128)(2,1)S(1)}, u32[]{:S(2)}, u32[]{:S(2)}) collective-permute-start(bf16[128,2048]{1,0:T(8,128)(2,1)} %get-tuple-element.137), channel_id=1, source_target_pairs={{0,1},{1,2},{2,3},{3,0},{4,5},{5,6},{6,7},{7,4},{8,9},{9,10},{10,1... | collective-permute-start | bytes 1572872 | tf_op jit(solution)/shard_map/ppermute | solution.py:607
  124.7 24.6 %collective-permute-start.5 = (bf16[128,2048]{1,0:T(8,128)(2,1)S(1)}, bf16[128,2048]{1,0:T(8,128)(2,1)S(1)}, u32[]{:S(2)}, u32[]{:S(2)}) collective-permute-start(bf16[128,2048]{1,0:T(8,128)(2,1)S(1)} %copy-done.21), channel_id=1, source_target_pairs={{0,4},{4,0},{1,5},{5,1},{2,6},{6,2},{3,7},{7,3},{8,12},{12,8},{9,1... | collective-permute-start | bytes 1572872 | tf_op jit(solution)/shard_map/ppermute | solution.py:607
  124.8 29.7 %collective-permute-start.6 = (bf16[128,2048]{1,0:T(8,128)(2,1)S(1)}, bf16[128,2048]{1,0:T(8,128)(2,1)S(1)}, u32[]{:S(2)}, u32[]{:S(2)}) collective-permute-start(bf16[128,2048]{1,0:T(8,128)(2,1)S(1)} %copy-done.20), channel_id=1, source_target_pairs={{0,3},{1,0},{2,1},{3,2},{4,7},{5,4},{6,5},{7,6},{8,11},{9,8},{10,9... | collective-permute-start | bytes 1572872 | tf_op jit(solution)/shard_map/ppermute | solution.py:607
  147.7 10.6 %copy-start.19 = (bf16[128,2048]{1,0:T(8,128)(2,1)S(1)}, bf16[128,2048]{1,0:T(8,128)(2,1)}, u32[]{:S(2)}) copy-start(bf16[128,2048]{1,0:T(8,128)(2,1)} %get-tuple-element.122) | copy-start | bytes 1572868
  149.3 5.2 %copy-start.6 = (bf16[128,2048]{1,0:T(8,128)(2,1)}, bf16[128,2048]{1,0:T(8,128)(2,1)S(1)}, u32[]{:S(2)}) copy-start(bf16[128,2048]{1,0:T(8,128)(2,1)S(1)} %collective-permute-done.4.refs_1_) | copy-start | bytes 1572868
  149.3 5.2 %copy-start.7 = (bf16[128,2048]{1,0:T(8,128)(2,1)}, bf16[128,2048]{1,0:T(8,128)(2,1)S(1)}, u32[]{:S(2)}) copy-start(bf16[128,2048]{1,0:T(8,128)(2,1)S(1)} %collective-permute-done.5.refs_2_) | copy-start | bytes 1572868
  154.5 0.8 copy-start.8
  158.3 3.8 %copy-start.23 = (bf16[128,2048]{1,0:T(8,128)(2,1)S(1)}, bf16[128,2048]{1,0:T(8,128)(2,1)}, u32[]{:S(2)}) copy-start(bf16[128,2048]{1,0:T(8,128)(2,1)} %get-tuple-element.150) | copy-start | bytes 1572868
  158.3 3.8 %copy-start.22 = (bf16[128,2048]{1,0:T(8,128)(2,1)S(1)}, bf16[128,2048]{1,0:T(8,128)(2,1)}, u32[]{:S(2)}) copy-start(bf16[128,2048]{1,0:T(8,128)(2,1)} %get-tuple-element.151) | copy-start | bytes 1572868
  158.3 24.8 %collective-permute-start.3 = (bf16[128,2048]{1,0:T(8,128)(2,1)S(1)}, bf16[128,2048]{1,0:T(8,128)(2,1)S(1)}, u32[]{:S(2)}, u32[]{:S(2)}) collective-permute-start(bf16[128,2048]{1,0:T(8,128)(2,1)S(1)} %copy-done.19), channel_id=1, source_target_pairs={{0,3},{1,0},{2,1},{3,2},{4,7},{5,4},{6,5},{7,6},{8,11},{9,8},{10,9... | collective-permute-start | bytes 1572872 | tf_op jit(solution)/shard_map/ppermute | solution.py:607
  162.1 24.6 %collective-permute-start.7 = (bf16[128,2048]{1,0:T(8,128)(2,1)S(1)}, bf16[128,2048]{1,0:T(8,128)(2,1)S(1)}, u32[]{:S(2)}, u32[]{:S(2)}) collective-permute-start(bf16[128,2048]{1,0:T(8,128)(2,1)S(1)} %copy-done.23), channel_id=1, source_target_pairs={{0,1},{1,2},{2,3},{3,0},{4,5},{5,6},{6,7},{7,4},{8,9},{9,10},{10,1... | collective-permute-start | bytes 1572872 | tf_op jit(solution)/shard_map/ppermute | solution.py:607
  162.1 26.8 %collective-permute-start.8 = (bf16[128,2048]{1,0:T(8,128)(2,1)S(1)}, bf16[128,2048]{1,0:T(8,128)(2,1)S(1)}, u32[]{:S(2)}, u32[]{:S(2)}) collective-permute-start(bf16[128,2048]{1,0:T(8,128)(2,1)S(1)} %copy-done.22), channel_id=1, source_target_pairs={{0,4},{4,0},{1,5},{5,1},{2,6},{6,2},{3,7},{7,3},{8,12},{12,8},{9,1... | collective-permute-start | bytes 1572872 | tf_op jit(solution)/shard_map/ppermute | solution.py:607
  183.1 14.2 %copy-start.9 = (bf16[128,2048]{1,0:T(8,128)(2,1)}, bf16[128,2048]{1,0:T(8,128)(2,1)S(1)}, u32[]{:S(2)}) copy-start(bf16[128,2048]{1,0:T(8,128)(2,1)S(1)} %collective-permute-done.3.refs_1_) | copy-start | bytes 1572868
  186.7 10.6 %copy-start.10 = (bf16[128,2048]{1,0:T(8,128)(2,1)}, bf16[128,2048]{1,0:T(8,128)(2,1)S(1)}, u32[]{:S(2)}) copy-start(bf16[128,2048]{1,0:T(8,128)(2,1)S(1)} %collective-permute-done.7.refs_2_) | copy-start | bytes 1572868
  188.9 8.3 %copy-start.11 = (bf16[128,2048]{1,0:T(8,128)(2,1)}, bf16[128,2048]{1,0:T(8,128)(2,1)S(1)}, u32[]{:S(2)}) copy-start(bf16[128,2048]{1,0:T(8,128)(2,1)S(1)} %collective-permute-done.8.refs_3_) | copy-start | bytes 1572868
  201.5 15.1 %collective-permute-start.11 = (bf16[128,2048]{1,0:T(8,128)(2,1)}, bf16[128,2048]{1,0:T(8,128)(2,1)S(1)}, u32[]{:S(2)}, u32[]{:S(2)}) collective-permute-start(bf16[128,2048]{1,0:T(8,128)(2,1)} %input.1.refs_0_), channel_id=1, source_target_pairs={{0,4},{4,0},{1,5},{5,1},{2,6},{6,2},{3,7},{7,3},{8,12},{12,8},{9,1... | collective-permute-start | bytes 1572872 | tf_op jit(solution)/shard_map/ppermute | solution.py:607
  203.4 14.3 %collective-permute-start.10 = (bf16[128,2048]{1,0:T(8,128)(2,1)}, bf16[128,2048]{1,0:T(8,128)(2,1)S(1)}, u32[]{:S(2)}, u32[]{:S(2)}) collective-permute-start(bf16[128,2048]{1,0:T(8,128)(2,1)} %input.1.refs_0_), channel_id=1, source_target_pairs={{0,3},{1,0},{2,1},{3,2},{4,7},{5,4},{6,5},{7,6},{8,11},{9,8},{10,9... | collective-permute-start | bytes 1572872 | tf_op jit(solution)/shard_map/ppermute | solution.py:607
  207.7 13.4 %collective-permute-start.9 = (bf16[128,2048]{1,0:T(8,128)(2,1)}, bf16[128,2048]{1,0:T(8,128)(2,1)S(1)}, u32[]{:S(2)}, u32[]{:S(2)}) collective-permute-start(bf16[128,2048]{1,0:T(8,128)(2,1)} %input.1.refs_0_), channel_id=1, source_target_pairs={{0,1},{1,2},{2,3},{3,0},{4,5},{5,6},{6,7},{7,4},{8,9},{9,10},{10,1... | collective-permute-start | bytes 1572872 | tf_op jit(solution)/shard_map/ppermute | solution.py:607
  209.5 18.5 %collective-permute-start.15 = (bf16[128,1920]{1,0:T(8,128)(2,1)}, bf16[128,1920]{1,0:T(8,128)(2,1)}, u32[]{:S(2)}, u32[]{:S(2)}) collective-permute-start(bf16[128,1920]{1,0:T(8,128)(2,1)} %slice.33), channel_id=1, source_target_pairs={{0,64},{64,0},{1,65},{65,1},{2,66},{66,2},{3,67},{67,3},{4,68},{68... | collective-permute-start | bytes 1474568 | tf_op jit(solution)/shard_map/ppermute | solution.py:607
  216.5 41.9 %copy-start.3 = (bf16[128,2048]{1,0:T(8,128)(2,1)}, bf16[128,2048]{1,0:T(8,128)(2,1)S(1)}, u32[]{:S(2)}) copy-start(bf16[128,2048]{1,0:T(8,128)(2,1)S(1)} %collective-permute-done.11.refs_3_) | copy-start | bytes 1572868
  217.7 40.7 %copy-start.4 = (bf16[128,2048]{1,0:T(8,128)(2,1)}, bf16[128,2048]{1,0:T(8,128)(2,1)S(1)}, u32[]{:S(2)}) copy-start(bf16[128,2048]{1,0:T(8,128)(2,1)S(1)} %collective-permute-done.10.refs_2_) | copy-start | bytes 1572868
  221.0 37.4 %copy-start.5 = (bf16[128,2048]{1,0:T(8,128)(2,1)}, bf16[128,2048]{1,0:T(8,128)(2,1)S(1)}, u32[]{:S(2)}) copy-start(bf16[128,2048]{1,0:T(8,128)(2,1)S(1)} %collective-permute-done.9.refs_1_) | copy-start | bytes 1572868
  221.1 31.9 %collective-permute-start.13 = (bf16[128,2048]{1,0:T(8,128)(2,1)S(1)}, bf16[128,2048]{1,0:T(8,128)(2,1)S(1)}, u32[]{:S(2)}, u32[]{:S(2)}) collective-permute-start(bf16[128,2048]{1,0:T(8,128)(2,1)S(1)} %collective-permute-done.10.refs_2_), channel_id=1, source_target_pairs={{0,4},{4,0},{1,5},{5,1},{2,6},{6,2},{3,7},{7,3},{8,12},{12,8},{9,1... | collective-permute-start | bytes 1572872 | tf_op jit(solution)/shard_map/ppermute | solution.py:607
  222.6 30.3 %collective-permute-start.12 = (bf16[128,2048]{1,0:T(8,128)(2,1)S(1)}, bf16[128,2048]{1,0:T(8,128)(2,1)S(1)}, u32[]{:S(2)}, u32[]{:S(2)}) collective-permute-start(bf16[128,2048]{1,0:T(8,128)(2,1)S(1)} %collective-permute-done.10.refs_2_), channel_id=1, source_target_pairs={{0,3},{1,0},{2,1},{3,2},{4,7},{5,4},{6,5},{7,6},{8,11},{9,8},{10,9... | collective-permute-start | bytes 1572872 | tf_op jit(solution)/shard_map/ppermute | solution.py:607
  223.3 29.7 %collective-permute-start.14 = (bf16[128,2048]{1,0:T(8,128)(2,1)S(1)}, bf16[128,2048]{1,0:T(8,128)(2,1)S(1)}, u32[]{:S(2)}, u32[]{:S(2)}) collective-permute-start(bf16[128,2048]{1,0:T(8,128)(2,1)S(1)} %collective-permute-done.11.refs_3_), channel_id=1, source_target_pairs={{0,1},{1,2},{2,3},{3,0},{4,5},{5,6},{6,7},{7,4},{8,9},{9,10},{10,1... | collective-permute-start | bytes 1572872 | tf_op jit(solution)/shard_map/ppermute | solution.py:607
  225.7 36.7 %collective-permute-start.19 = (bf16[128,1280]{1,0:T(8,128)(2,1)S(1)}, bf16[128,1280]{1,0:T(8,128)(2,1)}, u32[]{:S(2)}, u32[]{:S(2)}) collective-permute-start(bf16[128,1280]{1,0:T(8,128)(2,1)S(1)} %slice.38), channel_id=1, source_target_pairs={{0,64},{64,0},{1,65},{65,1},{2,66},{66,2},{3,67},{67,3},{4,68},{68... | collective-permute-start | bytes 983048 | tf_op jit(solution)/shard_map/ppermute | solution.py:607
  230.9 36.3 %copy-start.24 = (f32[128]{0:T(128)}, f32[128]{0:T(128)S(1)}, u32[]{:S(2)}) copy-start(f32[128]{0:T(128)S(1)} %slice_bitcast_fusion.1) | copy-start | bytes 1540
  253.0 5.5 %copy-start.2 = (bf16[128,2048]{1,0:T(8,128)(2,1)}, bf16[128,2048]{1,0:T(8,128)(2,1)S(1)}, u32[]{:S(2)}) copy-start(bf16[128,2048]{1,0:T(8,128)(2,1)S(1)} %collective-permute-done.14.refs_6_) | copy-start | bytes 1572868
  253.0 5.5 %copy-start = (bf16[128,2048]{1,0:T(8,128)(2,1)}, bf16[128,2048]{1,0:T(8,128)(2,1)S(1)}, u32[]{:S(2)}) copy-start(bf16[128,2048]{1,0:T(8,128)(2,1)S(1)} %collective-permute-done.13.refs_5_) | copy-start | bytes 1572868
  253.0 5.5 %copy-start.1 = (bf16[128,2048]{1,0:T(8,128)(2,1)}, bf16[128,2048]{1,0:T(8,128)(2,1)S(1)}, u32[]{:S(2)}) copy-start(bf16[128,2048]{1,0:T(8,128)(2,1)S(1)} %collective-permute-done.12.refs_4_) | copy-start | bytes 1572868
  253.0 11.5 %collective-permute-start.18 = (bf16[32,2048]{1,0:T(8,128)(2,1)S(1)}, bf16[32,2048]{1,0:T(8,128)(2,1)S(1)}, u32[]{:S(2)}, u32[]{:S(2)}) collective-permute-start(bf16[32,2048]{1,0:T(8,128)(2,1)S(1)} %slice.37), channel_id=1, source_target_pairs={{0,1},{1,2},{2,3},{3,0},{4,5},{5,6},{6,7},{7,4},{8,9},{9,10},{10,1... | collective-permute-start | bytes 393224 | tf_op jit(solution)/shard_map/ppermute | solution.py:607
  253.1 11.4 %collective-permute-start.17 = (bf16[48,2048]{1,0:T(8,128)(2,1)S(1)}, bf16[48,2048]{1,0:T(8,128)(2,1)S(1)}, u32[]{:S(2)}, u32[]{:S(2)}) collective-permute-start(bf16[48,2048]{1,0:T(8,128)(2,1)S(1)} %slice.36), channel_id=1, source_target_pairs={{0,3},{1,0},{2,1},{3,2},{4,7},{5,4},{6,5},{7,6},{8,11},{9,8},{10,9... | collective-permute-start | bytes 589832 | tf_op jit(solution)/shard_map/ppermute | solution.py:607
  256.4 8.1 %collective-permute-start.16 = (bf16[48,2048]{1,0:T(8,128)(2,1)S(1)}, bf16[48,2048]{1,0:T(8,128)(2,1)S(1)}, u32[]{:S(2)}, u32[]{:S(2)}) collective-permute-start(bf16[48,2048]{1,0:T(8,128)(2,1)S(1)} %slice.35), channel_id=1, source_target_pairs={{0,4},{4,0},{1,5},{5,1},{2,6},{6,2},{3,7},{7,3},{8,12},{12,8},{9,1... | collective-permute-start | bytes 589832 | tf_op jit(solution)/shard_map/ppermute | solution.py:607
  264.5 0.6 copy-start.16
  264.5 0.7 copy-start.14
  264.5 0.8 copy-start.15
Sparse Core Ops, SparseCore 0:
  70.5 126.7 all-reduce.3
Sparse Core Ops, SparseCore 1:
  123.8 57.6 reduce-scatter.2
  183.7 40.1 reduce-scatter.4
